TPU v7x, 32 devices: a whole 2x2x4 slice. The times are simulated.
32 devices in a mesh: replica: 2 (over y), dp: 4 (over x, core), tensor: 4 (over z).
Axes of the slice: x: 2, y: 2, z: 4, core: 2. Of those that a mesh axis runs over, the one named last changes fastest.
Arguments:
- hidden: bfloat16 [3, 1536, 8192], P(None, ('replica', 'dp'), 'tensor'), parts along dimension 1, may hold values from -6 to 6
- w_query: bfloat16 [8192, 4096], P(None, 'tensor'), may hold values from -0.0625 to 0.0625
- a_codes: bfloat16 [48, 8192, 128], P('dp', 'tensor'), may hold values from -0.0625 to 0.0625
- a_scales: float32 [48, 8192], P('dp', 'tensor'), may hold values from 0.5 to 2
- b_codes: bfloat16 [48, 128, 4096], P('dp', None, 'tensor'), may hold values from -0.5 to 0.5
- b_scales: float32 [48, 128], P('dp'), may hold values from 0.5 to 2
- variant_lists: int32 [8, 8], P('replica'), parts along dimension 0, may hold values from 0 to 47, as said below
- row_pick: int32 [1536], P(('replica', 'dp')), parts along dimension 0, may hold values from 0 to 7
- lengths: int32 [1536], P(('replica', 'dp', 'tensor')), parts along dimension 0, may hold values from 1 to 128, as said below
- page_table: int32 [1536, 8], P(('replica', 'dp', 'tensor')), parts along dimension 0, may hold values from 0 to 383, as said below
- new_kv: bfloat16 [3, 1536, 1024], P(None, ('replica', 'dp', 'tensor')), parts along dimension 1, may hold values from -6 to 6
- kv_cache: bfloat16 [12288, 16, 1024], P(('replica', 'dp', 'tensor')), parts along dimension 0
Outputs:
- attended: bfloat16 [3, 1536, 4096], P(None, ('replica', 'dp', 'tensor')), parts along dimension 1
There are 2 independent parts, one for each index of `replica`. A program takes and returns all parts, laid end to end along the dimension named above; an argument that names none is the same for every part. Nothing has to cross between parts.
Inputs may be any that keep to these rules, and one draw needn't show every extreme that they name: `variant_lists`: in each group the 8 variants are distinct. Variant v is owned by block v // 12; no block holds more than 2 of one group's variants, and in every group some block holds exactly 2. `lengths`: some row has exactly 128 cached tokens. `page_table`: within each aligned block b of 48 rows the 384 entries are distinct and name the pages b * 384 + entry of the pool; entries past a row's length are not read.
All inputs are finite; a program needn't handle non-finite values.
Results may differ from a plain program's by a relative error of at most 0.015.
The roundings to bfloat16 on the way count: a program that leaves them out, or rounds other values in their place, can miss the bound.
Values may be sent and summed in bfloat16 or wider, within the bound.
A program may use at most 192 MiB of HBM per device.

v0:
```python
import jax
import jax.numpy as jnp
from jax import lax
from jax.sharding import PartitionSpec as P

HEADS = 32
KVH = 4
HD = 128
CTX = 128


def dequant(code_block, scale_rows):
    return (code_block.astype(jnp.float32) * scale_rows[:, :, None]).astype(jnp.bfloat16)


def attend(queries, fresh_kv, row_lengths, row_table, pool_pages):
    n_steps, row_count, col_total = queries.shape
    share_count = HEADS // KVH
    pages_all = jnp.take(pool_pages, row_table.reshape(-1), axis=0).reshape(
        row_count, CTX, 2, KVH, HD
    )
    fresh_all = fresh_kv.reshape(n_steps, row_count, 2, KVH, HD)
    grouped = queries.reshape(n_steps, row_count, KVH, share_count, HD)
    inv_scale = HD ** (-0.5)
    score_old = (
        jnp.einsum(
            "trkgd,rskd->trkgs", grouped, pages_all[:, :, 0], preferred_element_type=jnp.float32
        )
        * inv_scale
    )
    score_new = (
        jnp.einsum(
            "trkgd,urkd->trkgu", grouped, fresh_all[:, :, 0], preferred_element_type=jnp.float32
        )
        * inv_scale
    )
    live_old = jnp.arange(CTX, dtype=jnp.int32)[None, :] < row_lengths[:, None]
    live_new = (
        jnp.arange(n_steps, dtype=jnp.int32)[None, :]
        <= jnp.arange(n_steps, dtype=jnp.int32)[:, None]
    )
    score_old = jnp.where(live_old[None, :, None, None, :], score_old, -1e30)
    score_new = jnp.where(live_new[:, None, None, None, :], score_new, -1e30)
    row_peak = jnp.maximum(jnp.max(score_old, axis=-1), jnp.max(score_new, axis=-1))
    exp_old = jnp.exp(score_old - row_peak[..., None])
    exp_new = jnp.exp(score_new - row_peak[..., None])
    denominator = jnp.sum(exp_old, axis=-1) + jnp.sum(exp_new, axis=-1)
    weight_old = (exp_old / denominator[..., None]).astype(jnp.bfloat16)
    weight_new = (exp_new / denominator[..., None]).astype(jnp.bfloat16)
    output = jnp.einsum(
        "trkgs,rskd->trkgd", weight_old, pages_all[:, :, 1], preferred_element_type=jnp.float32
    )
    output = output + jnp.einsum(
        "trkgu,urkd->trkgd", weight_new, fresh_all[:, :, 1], preferred_element_type=jnp.float32
    )
    return output.reshape(n_steps, row_count, col_total).astype(jnp.bfloat16)


def on_device(
    hidden,
    w_query,
    a_codes,
    a_scales,
    b_codes,
    b_scales,
    variant_lists,
    row_pick,
    lengths,
    page_table,
    new_kv,
    kv_cache,
):
    n_steps, n_rows, width_dev = hidden.shape
    col_count = w_query.shape[1]
    rank_size = a_codes.shape[2]
    list_size = variant_lists.shape[1]
    group_index = lax.axis_index("dp")
    a_own = dequant(a_codes, a_scales)
    b_own = dequant(b_codes, b_scales)
    own_list = lax.dynamic_index_in_dim(variant_lists, group_index, 0, keepdims=False)
    a_every, b_every = (
        lax.all_gather(a_own, "dp", axis=0, tiled=True),
        lax.all_gather(b_own, "dp", axis=0, tiled=True),
    )
    a_select = jnp.take(a_every, own_list, axis=0)
    b_select = jnp.take(b_every, own_list, axis=0)
    flattened = hidden.reshape(n_steps * n_rows, width_dev)
    base_part = jnp.dot(
        lax.all_gather(flattened, "tensor", axis=1, tiled=True),
        w_query,
        preferred_element_type=jnp.float32,
    )
    onehot = row_pick[:, None] == jnp.arange(list_size, dtype=jnp.int32)[None, :]
    low_all = jnp.einsum("trd,kdc->trkc", hidden, a_select, preferred_element_type=jnp.float32)
    low_part = jnp.sum(jnp.where(onehot[None, :, :, None], low_all, 0.0), axis=2)
    low_sum = lax.psum(low_part, "tensor")
    low_bf = low_sum.astype(jnp.bfloat16)
    spread = jnp.where(onehot[None, :, :, None], low_bf[:, :, None, :], jnp.zeros((), jnp.bfloat16))
    delta_q = jnp.dot(
        spread.reshape(n_steps * n_rows, list_size * rank_size),
        b_select.reshape(list_size * rank_size, col_count),
        preferred_element_type=jnp.float32,
    )
    queries = (base_part + delta_q).astype(jnp.bfloat16).reshape(n_steps, n_rows, col_count)
    by_rows = lax.all_to_all(queries, "tensor", split_axis=1, concat_axis=2, tiled=True)
    return attend(by_rows, new_kv, lengths, page_table, kv_cache)


def solution(mesh):
    placed = (
        P(None, ("replica", "dp"), "tensor"),
        P(None, "tensor"),
        P("dp", "tensor", None),
        P("dp", "tensor"),
        P("dp", None, "tensor"),
        P("dp", None),
        P("replica", None),
        P(("replica", "dp")),
        P(("replica", "dp", "tensor")),
        P(("replica", "dp", "tensor"), None),
        P(None, ("replica", "dp", "tensor"), None),
        P(("replica", "dp", "tensor"), None, None),
    )
    return jax.shard_map(
        on_device,
        mesh=mesh,
        in_specs=placed,
        out_specs=P(None, ("replica", "dp", "tensor"), None),
        check_vma=False,
    )
```

profile of v0, /device:TPU:0, one launch (start us, length us, event | category | flops | bytes accessed | tf_op | source)
XLA Modules:
  0.0 529.3 jit_solution(3300369781794097356)
XLA Ops:
  6.5 0.0 all-gather.8.cloned.1.call-start
  6.5 4.1 multiply_convert_fusion.1
  10.6 0.0 copy-start.3
  10.6 0.0 all-gather.8.cloned.1.call-update
  10.7 0.0 all-gather.6.cloned.1.call-start
  10.7 0.8 copy-done.3
  11.5 8.2 %multiply_convert_fusion = bf16[12,2048,128]{2,1,0:T(8,128)(2,1)} fusion(bf16[12,2048,128]{2,1,0:T(8,128)(2,1)} %param.14, f32[12,2048]{1,0:T(8,128)S(1)} %copy-done.3), kind=kLoop, calls=%fused_computation.4 | loop fusion | flops 9437184 | bytes 12681216 | tf_op jit(solution)/shard_map/convert_element_type | solution.py:13
  19.8 0.0 all-gather.6.cloned.1.call-update
  19.8 0.0 copy-start.4
  19.8 0.0 copy-start.7
  19.8 0.0 copy-start.5
  19.8 0.0 all-gather.4.cloned.1.call-start
  19.9 0.7 all-gather.4.cloned.1.call-update
  20.6 0.0 copy-done.4
  20.6 0.1 copy.25
  20.7 0.1 reshape.200
  20.7 0.0 copy-done.7
  20.8 0.0 copy-done.5
  20.9 74.8 %all-gather.8.cloned.1.call-done = bf16[48,128,1024]{2,1,0:T(8,128)(2,1)} async-done(((bf16[12,128,1024]{2,1,0:T(8,128)(2,1)}), bf16[48,128,1024]{2,1,0:T(8,128)(2,1)}) %all-gather.8.cloned.1.call-update) | async-done | bytes 12582928 | tf_op jit(solution)/shard_map/all_gather | solution.py:83
  95.6 5.3 gather_fusion.2
  100.9 1.6 broadcast_select_fusion
  102.5 0.0 copy-start
  102.5 149.5 %all-gather.6.cloned.1.call-done = bf16[48,2048,128]{2,1,0:T(8,128)(2,1)} async-done(((bf16[12,2048,128]{2,1,0:T(8,128)(2,1)}), bf16[48,2048,128]{2,1,0:T(8,128)(2,1)}) %all-gather.6.cloned.1.call-update) | async-done | bytes 25165840 | tf_op jit(solution)/shard_map/all_gather | solution.py:82
  252.0 11.4 %gather_fusion.1 = bf16[8,2048,128]{2,1,0:T(8,128)(2,1)} fusion(bf16[48,2048,128]{2,1,0:T(8,128)(2,1)} %all-gather.6.cloned.1.call-done, s32[1024]{0:T(1024)S(1)} %pad_clamp_fusion), kind=kCustom, calls=%fused_computation.1 | custom fusion | bytes 8388640 | tf_op jit(solution)/shard_map/jit(_take)/gather | solution.py:85
  263.4 0.0 copy-done
  263.4 5.3 fusion.8
  268.7 0.0 copy-start.1
  268.7 38.6 %all-reduce.1 = bf16[3,192,128]{2,1,0:T(8,128)(2,1)S(1)} all-reduce(f32[3,192,128]{2,1,0:T(8,128)S(1)} %fusion.8), channel_id=1, replica_groups=mesh['replica'=2,'dp'=4,'tensor'=4] {'tensor'}, use_global_device_ids=true, to_apply=%region_1.2 | all-reduce | flops 73728 | bytes 442368 | tf_op jit(solution)/shard_map/psum | solution.py:96
  307.3 0.3 broadcast_select_fusion.1
  307.6 0.8 copy.27
  308.3 0.0 copy-done.1
  308.3 2.8 fusion.14
  311.1 118.6 %all-gather.4.cloned.1.call-done = bf16[576,8192]{1,0:T(8,128)(2,1)} async-done(((bf16[576,2048]{1,0:T(8,128)(2,1)}), bf16[576,8192]{1,0:T(8,128)(2,1)}) %all-gather.4.cloned.1.call-update) | async-done | bytes 9437200 | tf_op jit(solution)/shard_map/all_gather | solution.py:89
  429.8 16.6 %add_convert_fusion = bf16[576,1024]{1,0:T(8,128)(2,1)S(1)} fusion(f32[576,1024]{1,0:T(8,128)} %fusion.14, bf16[576,8192]{1,0:T(8,128)(2,1)} %all-gather.4.cloned.1.call-done, bf16[8192,1024]{1,0:T(8,128)(2,1)} %param.13), kind=kOutput, calls=%fused_computation.24 | convolution fusion | flops 9664856064 | bytes 29753344 | tf_op jit(solution)/shard_map/dot_general | solution.py:88
  446.4 2.2 copy.28
  448.7 3.7 all-to-all-start
  452.4 15.9 %gather_fusion = bf16[384,16,1024]{2,1,0:T(8,128)(2,1)} fusion(bf16[384,16,1024]{2,1,0:T(8,128)(2,1)} %param.23, s32[1024]{0:T(1024)S(1)} %pad_clamp_fusion.1), kind=kCustom, calls=%fused_computation | custom fusion | bytes 25167360 | tf_op jit(solution)/shard_map/jit(_take)/gather | solution.py:19
  468.3 20.8 %gather.15 = bf16[48,128,2,4,128]{4,3,2,1,0:T(4,128)(2,1)} reshape(bf16[384,16,1024]{2,1,0:T(8,128)(2,1)} %gather_fusion) | data formatting | bytes 25165824 | tf_op jit(solution)/shard_map/jit(_take)/gather | solution.py:19
  489.1 0.1 copy.24
  489.2 0.0 copy-done.2
  489.2 0.2 reshape.204
  489.4 0.0 copy-done.6
  489.5 0.1 iota_compare_fusion
  489.5 0.1 fusion.36
  489.6 11.7 %copy_select_fusion = bf16[48,128,2,4,128]{4,1,3,0,2:T(8,128)(2,1)} fusion(bf16[48,128,2,4,128]{4,3,2,1,0:T(4,128)(2,1)} %gather.15, pred[48,128]{1,0:T(8,128)(4,1)S(1)} %copy.24), kind=kLoop, calls=%fused_computation.3 | loop fusion | flops 6291456 | bytes 25171968 | tf_op jit(solution)/shard_map/jit(_take)/select_n | solution.py:19
  501.4 0.0 all-to-all-done
  501.4 0.4 copy.29
  501.8 0.3 copy.43
  502.1 0.0 slice-start
  502.1 0.0 slice-start.1
  502.1 6.2 %bitcast_reduce_fusion = (f32[3,48,4,8]{3,0,2,1:T(4,128)S(1)}, f32[48,4,128,3,8]{2,4,3,1,0:T(8,128)S(1)}) fusion(pred[48,128]{1,0:T(8,128)(4,1)S(1)} %iota_compare_fusion, bf16[3,48,4,8,128]{4,3,1,2,0:T(8,128)(2,1)S(1)} %bitcast.97, bf16[48,128,2,4,128]{4,1,3,0,2:T(8,128)(2,1)} %copy_select_fusion), kind=kOutput, calls=%fused_computation.17 | convolution fusion | flops 152759808 | bytes 9854976 | tf_op jit(solution)/shard_map/trkgd,rskd->trkgs/dot_general | solution.py:26
  508.4 0.0 slice-start.2
  508.4 3.9 fusion.37
  512.3 0.1 max.7
  512.4 1.1 fusion.28
  513.5 1.6 fusion.11
  515.1 0.1 add.66
  515.2 0.0 slice-done
  515.2 0.0 slice-done.1
  515.2 0.0 slice-done.2
  515.3 3.4 fusion.1
  518.7 2.5 fusion.6
  521.2 0.2 copy.34
  521.4 1.4 convert_element_type.39
  (12 shorter events, 0.1 us)
Async XLA Ops:
  6.5 89.1 %all-gather.8.cloned.1.call-start = ((), (), s32[]{:S(2)}) async-start(), calls=%async_computation.3 | async-start | bytes 15728640 | tf_op jit(solution)/shard_map/all_gather | solution.py:83
  10.6 0.9 copy-start.3
  10.7 241.4 %all-gather.6.cloned.1.call-start = ((), (), s32[]{:S(2)}) async-start(), calls=%async_computation.2 | async-start | bytes 31457280 | tf_op jit(solution)/shard_map/all_gather | solution.py:82
  19.8 0.8 copy-start.4
  19.8 1.0 copy-start.7
  19.8 1.0 copy-start.5
  19.8 409.9 %all-gather.4.cloned.1.call-start = ((), (), s32[]{:S(2)}) async-start(), calls=%async_computation.1 | async-start | bytes 11796480 | tf_op jit(solution)/shard_map/all_gather | solution.py:89
  102.5 161.0 %copy-start = (bf16[3,192,2048]{2,1,0:T(8,128)(2,1)S(1)}, bf16[3,192,2048]{2,1,0:T(8,128)(2,1)}, u32[]{:S(2)}) copy-start(bf16[3,192,2048]{2,1,0:T(8,128)(2,1)} %param.12) | copy-start | bytes 7077892
  268.7 39.6 %copy-start.1 = (bf16[8,128,1024]{2,1,0:T(8,128)(2,1)S(1)}, bf16[8,128,1024]{2,1,0:T(8,128)(2,1)}, u32[]{:S(2)}) copy-start(bf16[8,128,1024]{2,1,0:T(8,128)(2,1)} %broadcast_select_fusion) | copy-start | bytes 6291460
  448.7 52.7 %all-to-all-start = ((bf16[3,192,1024]{2,0,1:T(4,128)(2,1)}), bf16[3,192,1024]{2,0,1:T(4,128)(2,1)S(1)}, u32[]{:S(2)}, u32[]{:S(2)}) async-start(bf16[3,192,1024]{2,0,1:T(4,128)(2,1)} %copy.28), calls=%async_computation | async-start | bytes 3145728 | tf_op jit(solution)/shard_map/all_to_all | solution.py:105
  468.3 21.0 %copy-start.2 = (bf16[3,48,1024]{2,1,0:T(8,128)(2,1)S(1)}, bf16[3,48,1024]{2,1,0:T(8,128)(2,1)}, u32[]{:S(2)}) copy-start(bf16[3,48,1024]{2,1,0:T(8,128)(2,1)} %param.22) | copy-start | bytes 884740
  468.3 21.2 %copy-start.6 = (s32[48]{0:T(128)S(1)}, s32[48]{0:T(128)}, u32[]{:S(2)}) copy-start(s32[48]{0:T(128)} %param.20) | copy-start | bytes 580
  502.1 13.1 %slice-start = ((s8[12582912]{0:T(1024)(128)(4,1)}), s8[4194304]{0:T(1024)(128)(4,1)S(1)}, s32[]{:S(2)}) async-start(s8[12582912]{0:T(1024)(128)(4,1)} %bitcast.91), calls=%async_computation.4 | async-start | bytes 8388608
  502.1 13.1 %slice-start.1 = ((s8[12582912]{0:T(1024)(128)(4,1)}), s8[4194304]{0:T(1024)(128)(4,1)S(1)}, s32[]{:S(2)}) async-start(s8[12582912]{0:T(1024)(128)(4,1)} %bitcast.91), calls=%async_computation.5 | async-start | bytes 8388608
  508.4 6.9 %slice-start.2 = ((s8[12582912]{0:T(1024)(128)(4,1)}), s8[4194304]{0:T(1024)(128)(4,1)S(1)}, s32[]{:S(2)}) async-start(s8[12582912]{0:T(1024)(128)(4,1)} %bitcast.91), calls=%async_computation.6 | async-start | bytes 8388608
Sparse Core Ops, SparseCore 0:
  10.8 84.8 all-gather.7
  97.2 154.7 all-gather.5
  253.6 176.1 all-gather.3
where the time goes:
time: 530 us; the launch traced here: 529 us
  waiting for transfers between devices  344 us (65%)
  local copies, waits for them, and re-layouts  60.1 us (11%)
  matrix products  40.8 us (8%)
  blocking collectives  38.6 us (7%)
  other arithmetic  28.9 us (5%)
  between operations  13.4 us (3%)
    all_gather x1, waiting for transfers between devices, on_device(): lax.all_gather(a_own, 'dp', axis=0, tiled=True)  150 us
    all_gather x1, waiting for transfers between devices, on_device(): lax.all_gather(flattened, 'tensor', axis=1, tiled=True)  119 us
    all_gather x1, waiting for transfers between devices, on_device(): lax.all_gather(b_own, 'dp', axis=0, tiled=True)  74.8 us
    psum x1, blocking collectives, on_device(): low_sum = lax.psum(low_part, 'tensor')  38.6 us
    gather x2, local copies, waits for them, and re-layouts, attend(): jnp.take(pool_pages, row_table.reshape(-1), axis=0)  36.7 us
    dot_general x1, matrix products, on_device(): jnp.dot(lax.all_gather(flattened, 'tensor', axis=1, tiled=True), w_query,...  16.6 us
    convert_element_type x2, other arithmetic, dequant(): (code_block.astype(jnp.float32) * scale_rows[:, :, None]).astype(jnp.bflo...  12.3 us
    select_n x2, other arithmetic, attend(): jnp.take(pool_pages, row_table.reshape(-1), axis=0)  11.7 us
  transfers between devices with their start and end apart: 4, of which 3 were waited for; matrix products, arithmetic and copies ran while one was open for 16% of the time, Pallas kernels for 0%

commit v1 on v0

v1 whole, which is shorter than its diff:
```python
import functools

import jax
import jax.numpy as jnp
from jax import lax
from jax.experimental import pallas as pl
from jax.experimental.pallas import tpu as pltpu
from jax.sharding import PartitionSpec as P

HEADS = 32
KVH = 4
HD = 128
SLOTS = 2
SHARE = HEADS // KVH


def dequant(code_block, scale_rows):
    return (code_block.astype(jnp.float32) * scale_rows[..., None]).astype(jnp.bfloat16)


def attend_kernel(n_steps, len_ref, q_ref, kv_ref, new_ref, out_ref):
    inv_scale = HD ** (-0.5)
    ctx = kv_ref.shape[1]
    n_new = new_ref.shape[1]
    rows, q_rows = q_ref.shape[1], q_ref.shape[2]
    old_pos = lax.broadcasted_iota(jnp.int32, (rows, q_rows, ctx), 2)
    live_old = old_pos < len_ref[...]
    step = lax.broadcasted_iota(jnp.int32, (rows, q_rows, n_new), 1) // SHARE
    new_pos = lax.broadcasted_iota(jnp.int32, (rows, q_rows, n_new), 2)
    live_new = new_pos <= step
    qk = (((2,), (2,)), ((0,), (0,)))
    pv = (((2,), (1,)), ((0,), (0,)))
    for head in range(KVH):
        k_cols = pl.ds(head * HD, HD)
        v_cols = pl.ds((KVH + head) * HD, HD)
        q = q_ref[head]
        s_old = lax.dot_general(q, kv_ref[:, :, k_cols], qk, preferred_element_type=jnp.float32)
        s_new = lax.dot_general(q, new_ref[:, :, k_cols], qk, preferred_element_type=jnp.float32)
        s_old = jnp.where(live_old, s_old * inv_scale, -1e30)
        s_new = jnp.where(live_new, s_new * inv_scale, -1e30)
        peak = jnp.maximum(
            jnp.max(s_old, axis=-1, keepdims=True), jnp.max(s_new, axis=-1, keepdims=True)
        )
        e_old = jnp.exp(s_old - peak)
        e_new = jnp.exp(s_new - peak)
        inv = 1.0 / (
            jnp.sum(e_old, axis=-1, keepdims=True) + jnp.sum(e_new, axis=-1, keepdims=True)
        )
        p_old = (e_old * inv).astype(jnp.bfloat16)
        p_new = (e_new * inv).astype(jnp.bfloat16)
        out = lax.dot_general(p_old, kv_ref[:, :, v_cols], pv, preferred_element_type=jnp.float32)
        out += lax.dot_general(p_new, new_ref[:, :, v_cols], pv, preferred_element_type=jnp.float32)
        out_ref[head] = out.astype(jnp.bfloat16)


def attend(q, pages, fresh, row_lengths, n_steps):
    _, rows, q_rows, _ = q.shape
    ctx, kv_width = pages.shape[1:]
    n_new = fresh.shape[1]
    block = 8 if rows % 8 == 0 else rows
    lens = jnp.broadcast_to(row_lengths[:, None, None], (rows, 1, ctx))
    return pl.pallas_call(
        functools.partial(attend_kernel, n_steps),
        grid=(rows // block,),
        out_shape=jax.ShapeDtypeStruct(q.shape, jnp.bfloat16),
        in_specs=[
            pl.BlockSpec((block, 1, ctx), lambda i: (i, 0, 0)),
            pl.BlockSpec((KVH, block, q_rows, HD), lambda i: (0, i, 0, 0)),
            pl.BlockSpec((block, ctx, kv_width), lambda i: (i, 0, 0)),
            pl.BlockSpec((block, n_new, kv_width), lambda i: (i, 0, 0)),
        ],
        out_specs=pl.BlockSpec((KVH, block, q_rows, HD), lambda i: (0, i, 0, 0)),
        compiler_params=pltpu.CompilerParams(vmem_limit_bytes=32 * 1024 * 1024),
        cost_estimate=pl.CostEstimate(
            flops=4 * KVH * rows * q_rows * HD * ctx,
            bytes_accessed=pages.size * 2 + 2 * q.size * 2,
            transcendentals=KVH * rows * q_rows * ctx,
        ),
    )(lens, q, pages, fresh)


def on_device(
    hidden,
    w_query,
    a_codes,
    a_scales,
    b_codes,
    b_scales,
    variant_lists,
    row_pick,
    lengths,
    page_table,
    new_kv,
    kv_cache,
):
    n_steps, n_rows, width_dev = hidden.shape
    col_count = w_query.shape[1]
    owned, _, rank_size = a_codes.shape
    n_tensor = lax.axis_size("tensor")
    n_dp = lax.axis_size("dp")
    row_dev = lengths.shape[0]
    chunks = 3 if row_dev % 3 == 0 else 1
    row_chunk = row_dev // chunks
    group_index = lax.axis_index("dp")

    by_dev = hidden.reshape(n_steps, n_tensor, row_dev, width_dev)
    gathered = []
    for c in range(chunks):
        part = by_dev[:, :, c * row_chunk : (c + 1) * row_chunk]
        part = part.reshape(n_steps * n_tensor * row_chunk, width_dev)
        gathered.append(lax.all_gather(part, "tensor", axis=1, tiled=True))

    mine = variant_lists // owned == group_index
    rank_in = jnp.cumsum(mine.astype(jnp.int32), axis=1) - 1
    slot_ids = jnp.arange(SLOTS, dtype=jnp.int32)
    hit = mine[:, None, :] & (rank_in[:, None, :] == slot_ids[None, :, None])
    local = jnp.sum(jnp.where(hit, (variant_lists % owned)[:, None, :], 0), axis=2)
    picks = local.reshape(-1)
    a_send = dequant(
        a_codes.at[picks].get(mode="promise_in_bounds"),
        a_scales.at[picks].get(mode="promise_in_bounds"),
    ).reshape(n_dp, SLOTS, width_dev, rank_size)
    b_send = dequant(
        b_codes.at[picks].get(mode="promise_in_bounds"),
        b_scales.at[picks].get(mode="promise_in_bounds"),
    ).reshape(n_dp, SLOTS, rank_size, col_count)
    n_slots = n_dp * SLOTS
    a_select = lax.all_to_all(a_send, "dp", 0, 0, tiled=True).reshape(n_slots, width_dev, rank_size)
    b_select = lax.all_to_all(b_send, "dp", 0, 0, tiled=True).reshape(
        n_slots * rank_size, col_count
    )

    own_list = lax.dynamic_index_in_dim(variant_lists, group_index, 0, keepdims=False)
    owner = own_list // owned
    earlier = jnp.tril(jnp.ones((own_list.shape[0],) * 2, jnp.int32), -1)
    place = jnp.sum((owner[:, None] == owner[None, :]).astype(jnp.int32) * earlier, axis=1)
    slot_of = owner * SLOTS + place
    pick_hot = row_pick[:, None] == jnp.arange(own_list.shape[0], dtype=jnp.int32)[None, :]
    row_slot = jnp.sum(jnp.where(pick_hot, slot_of[None, :], 0), axis=1)
    onehot = row_slot[:, None] == jnp.arange(n_slots, dtype=jnp.int32)[None, :]

    low_all = jnp.einsum("trd,kdc->trkc", hidden, a_select, preferred_element_type=jnp.float32)
    low_part = jnp.sum(jnp.where(onehot[None, :, :, None], low_all, 0.0), axis=2)
    low_bf = lax.psum(low_part, "tensor").astype(jnp.bfloat16)
    spread = jnp.where(onehot[None, :, :, None], low_bf[:, :, None, :], jnp.zeros((), jnp.bfloat16))
    spread = spread.reshape(n_steps, n_tensor, row_dev, n_slots * rank_size)

    fresh = jnp.pad(new_kv.transpose(1, 0, 2), ((0, 0), (0, 16 - n_steps), (0, 0)))
    head_dev = col_count // HD
    outs = []
    for c in range(chunks):
        rows = slice(c * row_chunk, (c + 1) * row_chunk)
        pages = kv_cache.at[page_table[rows].reshape(-1)].get(mode="promise_in_bounds")
        pages = pages.reshape(row_chunk, -1, kv_cache.shape[2])
        base = jnp.dot(gathered[c], w_query, preferred_element_type=jnp.float32)
        delta = jnp.dot(
            spread[:, :, rows].reshape(-1, n_slots * rank_size),
            b_select,
            preferred_element_type=jnp.float32,
        )
        q = (base + delta).astype(jnp.bfloat16)
        q = q.reshape(n_steps, n_tensor, row_chunk, head_dev, HD).transpose(1, 2, 0, 3, 4)
        q = q.reshape(n_tensor, row_chunk, n_steps * head_dev, HD)
        q = lax.all_to_all(q, "tensor", 0, 0, tiled=True)
        q = q.reshape(KVH, n_tensor // KVH, row_chunk, n_steps, head_dev, HD)
        q = q.transpose(0, 2, 3, 1, 4, 5).reshape(KVH, row_chunk, n_steps * SHARE, HD)
        out = attend(q, pages, fresh[rows], lengths[rows], n_steps)
        out = out.reshape(KVH, row_chunk, n_steps, SHARE * HD).transpose(2, 1, 0, 3)
        outs.append(out.reshape(n_steps, row_chunk, HEADS * HD))
    return jnp.concatenate(outs, axis=1)


def solution(mesh):
    placed = (
        P(None, ("replica", "dp"), "tensor"),
        P(None, "tensor"),
        P("dp", "tensor", None),
        P("dp", "tensor"),
        P("dp", None, "tensor"),
        P("dp", None),
        P("replica", None),
        P(("replica", "dp")),
        P(("replica", "dp", "tensor")),
        P(("replica", "dp", "tensor"), None),
        P(None, ("replica", "dp", "tensor"), None),
        P(("replica", "dp", "tensor"), None, None),
    )
    return jax.shard_map(
        on_device,
        mesh=mesh,
        in_specs=placed,
        out_specs=P(None, ("replica", "dp", "tensor"), None),
        check_vma=False,
    )
```

time: 530 us -> 293 us (0.55)
  waiting for transfers between devices: 344 us -> 95.5 us
  other arithmetic: 28.9 us -> 12.2 us
  starting transfers between devices: 3.83 us -> 19.3 us
  Pallas kernels: 0 us -> 14.3 us
    all_gather x3, waiting for transfers between devices: 343 us -> 61.9 us  [on_device(): gathered.append(lax.all_gather(part, 'tensor', axis=1, tiled=True))]
    all_to_all x1 -> x5, waiting for transfers between devices: 0.01 us -> 32.2 us  [the longest x1 32.2 us: on_device(): lax.all_to_all(a_send, 'dp', 0, 0, tiled=True)]
    gather x4 -> x7, local copies, waits for them, and re-layouts: 53.4 us -> 31.4 us  [the longest x3 22.4 us: on_device(): kv_cache.at[page_table[rows].reshape(-1)].get(mode='promise_in_bounds')]
    all_to_all x1 -> x5, starting transfers between devices: 3.74 us -> 19.2 us  [the longest x3 10.6 us: on_device(): q = lax.all_to_all(q, 'tensor', 0, 0, tiled=True)]
    pallas_call x0 -> x3, Pallas kernels: none -> 14.3 us  [attend(): pl.pallas_call(functools.partial(attend_kernel, n_steps), grid=(rows // b...]
    select_n x4 -> x6, other arithmetic: 13.3 us -> 0.06 us  [the longest x1 0.02 us: on_device(): owner = own_list // owned]
    unnamed x24 -> x44, local copies, waits for them, and re-layouts: 1.27 us -> 12 us
    convert_element_type x2 -> x3, other arithmetic: 12.3 us -> 7.85 us  [the longest x2 7.83 us: dequant(): (code_block.astype(jnp.float32) * scale_rows[..., None]).astype(jnp.bfloa...]
  transfers between devices with their start and end apart: 4 -> 8, of which waited for: 3 -> 3; matrix products, arithmetic and copies ran while one was open for 16% -> 32% of each run, Pallas kernels for 0% -> 3%
where the time goes in v1:
time: 293 us; the launch traced here: 292 us
  waiting for transfers between devices  95.5 us (33%)
  local copies, waits for them, and re-layouts  63.6 us (22%)
  matrix products  37.7 us (13%)
  blocking collectives  36.2 us (12%)
  starting transfers between devices  19.3 us (7%)
  Pallas kernels  14.3 us (5%)
  between operations  13.5 us (5%)
  other arithmetic  12.2 us (4%)
    all_gather x3, waiting for transfers between devices, on_device(): gathered.append(lax.all_gather(part, 'tensor', axis=1, tiled=True))  61.9 us
    psum x1, blocking collectives, on_device(): low_bf = lax.psum(low_part, 'tensor').astype(jnp.bfloat16)  36.2 us
    all_to_all x1, waiting for transfers between devices, on_device(): lax.all_to_all(a_send, 'dp', 0, 0, tiled=True)  32.2 us
    dot_general x3, matrix products, on_device(): base = jnp.dot(gathered[c], w_query, preferred_element_type=jnp.float32)  28.3 us
    gather x3, local copies, waits for them, and re-layouts, on_device(): kv_cache.at[page_table[rows].reshape(-1)].get(mode='promise_in_bounds')  22.4 us
    pallas_call x3, Pallas kernels, attend(): pl.pallas_call(functools.partial(attend_kernel, n_steps), grid=(rows // b...  14.3 us
    unnamed x44, local copies, waits for them, and re-layouts  12 us
    all_to_all x3, starting transfers between devices, on_device(): q = lax.all_to_all(q, 'tensor', 0, 0, tiled=True)  10.6 us
  transfers between devices with their start and end apart: 8, of which 3 were waited for; matrix products, arithmetic and copies ran while one was open for 32% of the time, Pallas kernels for 3%

profile of v1, /device:TPU:0, one launch (start us, length us, event | category | flops | bytes accessed | tf_op | source)
XLA Modules:
  0.0 292.4 jit_solution(4007407746470900972)
XLA Ops:
  6.5 3.3 %fusion.24 = (bf16[3,4,16,2048]{3,2,1,0:T(8,128)(2,1)}, bf16[3,4,16,2048]{3,2,1,0:T(8,128)(2,1)}, bf16[3,4,16,2048]{3,2,1,0:T(8,128)(2,1)}) fusion(bf16[3,4,48,2048]{3,2,1,0:T(8,128)(2,1)} %bitcast.115), kind=kLoop, calls=%fused_computation.70 | loop fusion | bytes 4718592 | tf_op jit(solution)/shard_map/slice | solution.py:109
  9.9 0.7 all-gather.6.cloned.1.call-update
  10.7 0.2 reduce_window_sum.11
  10.9 0.1 select_reduce_fusion.1
  11.0 0.1 copy.44
  11.2 5.9 %gather_fusion = bf16[8,2048,128]{2,1,0:T(8,128)(2,1)} fusion(bf16[12,2048,128]{2,1,0:T(8,128)(2,1)} %param.14, s32[1024]{0:T(1024)S(1)} %pad_clamp_fusion.3), kind=kCustom, calls=%fused_computation | custom fusion | bytes 8388640 | tf_op jit(solution)/shard_map/gather | solution.py:120
  17.1 0.6 gather_fusion.1
  17.7 6.1 %fusion = bf16[4,2,2048,128]{3,2,1,0:T(8,128)(2,1)} fusion(bf16[4,2,2048,128]{3,2,1,0:T(8,128)(2,1)} %bitcast.110, f32[4,2,2048]{2,1,0:T(2,128)S(1)} %mul.31), kind=kLoop, calls=%fused_computation.8 | loop fusion | flops 6291456 | bytes 8454144 | tf_op jit(solution)/shard_map/convert_element_type | solution.py:18
  23.8 5.0 %all-to-all-start = ((bf16[4,2,2048,128]{3,2,1,0:T(8,128)(2,1)}), bf16[4,2,2048,128]{3,2,1,0:T(8,128)(2,1)}, u32[]{:S(2)}, u32[]{:S(2)}) async-start(bf16[4,2,2048,128]{3,2,1,0:T(8,128)(2,1)} %fusion), calls=%async_computation | async-start | bytes 8388608 | tf_op jit(solution)/shard_map/all_to_all | solution.py:128
  28.9 0.7 all-gather.8.cloned.1.call-update
  29.7 0.2 select_reduce_fusion.2
  30.0 0.1 copy.43
  30.1 0.4 copy-done.16
  30.6 0.3 broadcast_in_dim.118
  30.8 0.2 broadcast_in_dim.119
  31.1 2.0 gather_fusion.2
  33.1 0.6 gather_fusion.3
  33.9 2.0 copy.65
  36.2 7.6 %gather_fusion.4 = bf16[128,16,1024]{2,1,0:T(8,128)(2,1)} fusion(bf16[384,16,1024]{2,1,0:T(8,128)(2,1)} %param.23, s32[1024]{0:T(1024)S(1)} %pad_clamp_fusion.2), kind=kCustom, calls=%fused_computation.4 | custom fusion | bytes 8389120 | tf_op jit(solution)/shard_map/gather | solution.py:153
  43.7 1.7 fusion.1
  45.5 32.2 %all-to-all-done = bf16[4,2,2048,128]{3,2,1,0:T(8,128)(2,1)} async-done(((bf16[4,2,2048,128]{3,2,1,0:T(8,128)(2,1)}), bf16[4,2,2048,128]{3,2,1,0:T(8,128)(2,1)}, u32[]{:S(2)}, u32[]{:S(2)}) %all-to-all-start) | async-done | bytes 4194336 | tf_op jit(solution)/shard_map/all_to_all | solution.py:128
  77.7 3.6 %all-to-all-start.1 = ((bf16[4,2,128,1024]{3,2,1,0:T(8,128)(2,1)}), bf16[4,2,128,1024]{3,2,1,0:T(8,128)(2,1)S(1)}, u32[]{:S(2)}, u32[]{:S(2)}) async-start(bf16[4,2,128,1024]{3,2,1,0:T(8,128)(2,1)} %fusion.1), calls=%async_computation.1 | async-start | bytes 4194304 | tf_op jit(solution)/shard_map/all_to_all | solution.py:129
  81.3 6.0 %fusion.2 = f32[3,192,128]{2,1,0:T(8,128)S(1)} fusion(pred[192,8]{0,1:T(8,128)(4,1)S(1)} %copy-done.17, bf16[8,2048,128,1]{2,1,3,0:T(8,128)(2,1)} %bitcast.11, bf16[3,192,2048]{2,1,0:T(8,128)(2,1)} %param.12), kind=kOutput, calls=%fused_computation.15 | convolution fusion | flops 2417025024 | bytes 6850048 | tf_op jit(solution)/shard_map/trd,kdc->trkc/dot_general | solution.py:142
  87.3 36.2 %all-reduce.2 = bf16[3,192,128]{2,1,0:T(8,128)(2,1)S(1)} all-reduce(f32[3,192,128]{2,1,0:T(8,128)S(1)} %fusion.2), channel_id=1, replica_groups=mesh['replica'=2,'dp'=4,'tensor'=4] {'tensor'}, use_global_device_ids=true, to_apply=%region_5.6 | all-reduce | flops 73728 | bytes 442368 | tf_op jit(solution)/shard_map/psum | solution.py:144
  123.5 1.2 broadcast_in_dim.125
  124.7 3.0 %broadcast_in_dim.126 = bf16[3,4,48,1024]{3,2,1,0:T(8,128)(2,1)} reshape(bf16[3,192,8,128]{3,2,1,0:T(8,128)(2,1)} %broadcast_in_dim.125) | data formatting | bytes 2359296 | tf_op jit(solution)/shard_map/jit(_where)/broadcast_in_dim | solution.py:145
  127.7 1.4 broadcast_select_fusion
  129.2 0.1 fusion.25
  129.3 11.1 %fusion.28 = f32[192,1024]{1,0:T(8,128)} fusion(bf16[192,8192]{1,0:T(8,128)(2,1)} %all-gather.4.cloned.1.call-done, bf16[8192,1024]{1,0:T(8,128)(2,1)} %param.13), kind=kOutput, calls=%fused_computation.74 | convolution fusion | flops 3221225472 | bytes 20709376 | tf_op jit(solution)/shard_map/dot_general | solution.py:155
  140.4 2.3 fusion.10
  142.8 0.8 copy.66
  143.6 3.6 %all-to-all-start.2 = ((bf16[4,16,24,128]{3,2,1,0:T(8,128)(2,1)}), bf16[4,16,24,128]{3,2,1,0:T(8,128)(2,1)S(1)}, u32[]{:S(2)}, u32[]{:S(2)}) async-start(bf16[4,16,24,128]{3,2,1,0:T(8,128)(2,1)} %bitcast.122), calls=%async_computation.2 | async-start | bytes 786432 | tf_op jit(solution)/shard_map/all_to_all | solution.py:164
  147.2 3.9 %all-gather.6.cloned.1.call-done = bf16[192,8192]{1,0:T(8,128)(2,1)} async-done(((bf16[192,2048]{1,0:T(8,128)(2,1)}), bf16[192,8192]{1,0:T(8,128)(2,1)}) %all-gather.6.cloned.1.call-update) | async-done | bytes 3145744 | tf_op jit(solution)/shard_map/all_gather | solution.py:111
  151.1 8.6 %fusion.29 = f32[192,1024]{1,0:T(8,128)S(1)} fusion(bf16[192,8192]{1,0:T(8,128)(2,1)} %all-gather.6.cloned.1.call-done, bf16[8192,1024]{1,0:T(8,128)(2,1)} %param.13), kind=kOutput, calls=%fused_computation.75 | convolution fusion | flops 3221225472 | bytes 20709376 | tf_op jit(solution)/shard_map/dot_general | solution.py:155
  159.8 0.6 fusion.9
  160.4 0.8 copy.64
  161.3 3.5 %all-to-all-start.3 = ((bf16[4,16,24,128]{3,2,1,0:T(8,128)(2,1)}), bf16[4,16,24,128]{3,2,1,0:T(8,128)(2,1)S(1)}, u32[]{:S(2)}, u32[]{:S(2)}) async-start(bf16[4,16,24,128]{3,2,1,0:T(8,128)(2,1)} %bitcast.101), calls=%async_computation.3 | async-start | bytes 786432 | tf_op jit(solution)/shard_map/all_to_all | solution.py:164
  164.7 57.9 %all-gather.8.cloned.1.call-done = bf16[192,8192]{1,0:T(8,128)(2,1)} async-done(((bf16[192,2048]{1,0:T(8,128)(2,1)}), bf16[192,8192]{1,0:T(8,128)(2,1)}) %all-gather.8.cloned.1.call-update) | async-done | bytes 3145744 | tf_op jit(solution)/shard_map/all_gather | solution.py:111
  222.7 8.6 %fusion.30 = f32[192,1024]{1,0:T(8,128)S(1)} fusion(bf16[192,8192]{1,0:T(8,128)(2,1)} %all-gather.8.cloned.1.call-done, bf16[8192,1024]{1,0:T(8,128)(2,1)} %param.13), kind=kOutput, calls=%fused_computation.76 | convolution fusion | flops 3221225472 | bytes 20709376 | tf_op jit(solution)/shard_map/dot_general | solution.py:155
  231.3 0.6 fusion.8
  232.0 0.9 copy.63
  232.9 3.5 %all-to-all-start.4 = ((bf16[4,16,24,128]{3,2,1,0:T(8,128)(2,1)}), bf16[4,16,24,128]{3,2,1,0:T(8,128)(2,1)S(1)}, u32[]{:S(2)}, u32[]{:S(2)}) async-start(bf16[4,16,24,128]{3,2,1,0:T(8,128)(2,1)} %bitcast.100), calls=%async_computation.4 | async-start | bytes 786432 | tf_op jit(solution)/shard_map/all_to_all | solution.py:164
  236.3 7.4 %gather_fusion.5 = bf16[128,16,1024]{2,1,0:T(8,128)(2,1)} fusion(bf16[384,16,1024]{2,1,0:T(8,128)(2,1)} %param.23, s32[1024]{0:T(1024)S(1)} %pad_clamp_fusion.1), kind=kCustom, calls=%fused_computation.5 | custom fusion | bytes 8389120 | tf_op jit(solution)/shard_map/gather | solution.py:153
  243.7 7.5 %gather_fusion.6 = bf16[128,16,1024]{2,1,0:T(8,128)(2,1)} fusion(bf16[384,16,1024]{2,1,0:T(8,128)(2,1)} %param.23, s32[1024]{0:T(1024)S(1)} %pad_clamp_fusion), kind=kCustom, calls=%fused_computation.6 | custom fusion | bytes 8389120 | tf_op jit(solution)/shard_map/gather | solution.py:153
  251.2 1.0 pad_slice_fusion.2
  252.4 2.2 copy-done.2
  254.6 4.8 %shard_map.118 = bf16[4,16,24,128]{3,2,1,0:T(8,128)(2,1)S(1)} custom-call(s32[16,1,128]{2,1,0:T(1,128)S(1)} %broadcast_in_dim.112.len_ref, bf16[4,16,24,128]{3,2,1,0:T(8,128)(2,1)S(1)} %all-to-all-done.2.q_ref, bf16[16,128,1024]{2,1,0:T(8,128)(2,1)S(1)} %bitcast.104, bf16[16,16,1024]{2,1,0:T(8,128)(2,1)S(1)} %get-tuple-element.16.new_ref), custom_call_target="tpu_custom_call" | custom-call | flops 100663296 | bytes 4980736 | tf_op jit(solution)/shard_map/pallas_call | solution.py:62
  259.4 0.1 reshape.293
  259.5 0.4 copy.48
  259.9 1.0 reshape.294
  261.0 2.2 copy-done.4
  263.2 4.8 %shard_map.119 = bf16[4,16,24,128]{3,2,1,0:T(8,128)(2,1)S(1)} custom-call(s32[16,1,128]{2,1,0:T(1,128)S(1)} %broadcast_in_dim.128.len_ref, bf16[4,16,24,128]{3,2,1,0:T(8,128)(2,1)S(1)} %all-to-all-done.3.q_ref, bf16[16,128,1024]{2,1,0:T(8,128)(2,1)S(1)} %bitcast.106, bf16[16,16,1024]{2,1,0:T(8,128)(2,1)S(1)} %get-tuple-element.17.new_ref), custom_call_target="tpu_custom_call" | custom-call | flops 100663296 | bytes 4980736 | tf_op jit(solution)/shard_map/pallas_call | solution.py:62
  267.9 0.1 reshape.301
  268.0 0.4 copy.51
  268.4 1.0 reshape.302
  269.5 0.8 copy-done.6
  270.3 2.2 copy-done.3
  272.5 1.0 copy-done.5
  273.5 1.0 copy-done.7
  274.5 4.8 %shard_map.120 = bf16[4,16,24,128]{3,2,1,0:T(8,128)(2,1)S(1)} custom-call(s32[16,1,128]{2,1,0:T(1,128)S(1)} %broadcast_in_dim.129.len_ref, bf16[4,16,24,128]{3,2,1,0:T(8,128)(2,1)S(1)} %copy-done.7, bf16[16,128,1024]{2,1,0:T(8,128)(2,1)S(1)} %bitcast.105, bf16[16,16,1024]{2,1,0:T(8,128)(2,1)S(1)} %copy-done.5), custom_call_target="tpu_custom_call" | custom-call | flops 100663296 | bytes 4980736 | tf_op jit(solution)/shard_map/pallas_call | solution.py:62
  279.3 0.9 reshape.309
  280.2 2.2 copy.54
  282.4 1.3 reshape.310
  283.7 2.2 pad_maximum_fusion
  (73 shorter events, 1.6 us)
Async XLA Ops:
  6.5 24.5 %copy-start = (bf16[12,128,1024]{2,1,0:T(8,128)(2,1)S(1)}, bf16[12,128,1024]{2,1,0:T(8,128)(2,1)}, u32[]{:S(2)}) copy-start(bf16[12,128,1024]{2,1,0:T(8,128)(2,1)} %param.16) | copy-start | bytes 9437188
  6.5 122.8 %all-gather.4.cloned.1.call-start = ((), (), s32[]{:S(2)}) async-start(), calls=%async_computation.5 | async-start | bytes 3932160 | tf_op jit(solution)/shard_map/all_gather | solution.py:111
  6.5 4.1 %copy-start.15 = (s32[4,8]{1,0:T(4,128)S(1)}, s32[4,8]{1,0:T(4,128)}, u32[]{:S(2)}) copy-start(s32[4,8]{1,0:T(4,128)} %param.18) | copy-start | bytes 388
  9.9 141.3 %all-gather.6.cloned.1.call-start = ((), (), s32[]{:S(2)}) async-start(), calls=%async_computation.6 | async-start | bytes 3932160 | tf_op jit(solution)/shard_map/all_gather | solution.py:111
  11.2 5.9 %copy-start.11 = (f32[12,2048]{1,0:T(8,128)S(1)}, f32[12,2048]{1,0:T(8,128)}, u32[]{:S(2)}) copy-start(f32[12,2048]{1,0:T(8,128)} %param.15) | copy-start | bytes 294916
  23.8 6.1 %copy-start.19 = (s32[192]{0:T(256)S(1)}, s32[192]{0:T(256)}, u32[]{:S(2)}) copy-start(s32[192]{0:T(256)} %param.19) | copy-start | bytes 2308
  23.8 53.9 %all-to-all-start = ((bf16[4,2,2048,128]{3,2,1,0:T(8,128)(2,1)}), bf16[4,2,2048,128]{3,2,1,0:T(8,128)(2,1)}, u32[]{:S(2)}, u32[]{:S(2)}) async-start(bf16[4,2,2048,128]{3,2,1,0:T(8,128)(2,1)} %fusion), calls=%async_computation | async-start | bytes 8388608 | tf_op jit(solution)/shard_map/all_to_all | solution.py:128
  28.9 4.2 %copy-start.13 = (f32[12,128]{1,0:T(8,128)S(1)}, f32[12,128]{1,0:T(8,128)}, u32[]{:S(2)}) copy-start(f32[12,128]{1,0:T(8,128)} %param.17) | copy-start | bytes 18436
  28.9 4.7 %copy-start.14 = (s32[48,8]{0,1:T(8,128)S(1)}, s32[48,8]{0,1:T(8,128)}, u32[]{:S(2)}) copy-start(s32[48,8]{0,1:T(8,128)} %param.21) | copy-start | bytes 4612
  28.9 193.8 %all-gather.8.cloned.1.call-start = ((), (), s32[]{:S(2)}) async-start(), calls=%async_computation.7 | async-start | bytes 3932160 | tf_op jit(solution)/shard_map/all_gather | solution.py:111
  30.0 0.6 copy-start.16
  36.2 7.6 %copy-start.10 = (bf16[8,128,1024]{2,1,0:T(8,128)(2,1)S(1)}, bf16[8,128,1024]{2,1,0:T(8,128)(2,1)}, u32[]{:S(2)}) copy-start(bf16[8,128,1024]{2,1,0:T(8,128)(2,1)} %gather_fusion.2) | copy-start | bytes 6291460
  45.5 35.8 %copy-start.17 = (pred[192,8]{0,1:T(8,128)(4,1)S(1)}, pred[192,8]{0,1:T(8,128)(4,1)}, u32[]{:S(2)}) copy-start(pred[192,8]{0,1:T(8,128)(4,1)} %copy-done.16) | copy-start | bytes 4612
  77.7 62.7 %all-to-all-start.1 = ((bf16[4,2,128,1024]{3,2,1,0:T(8,128)(2,1)}), bf16[4,2,128,1024]{3,2,1,0:T(8,128)(2,1)S(1)}, u32[]{:S(2)}, u32[]{:S(2)}) async-start(bf16[4,2,128,1024]{3,2,1,0:T(8,128)(2,1)} %fusion.1), calls=%async_computation.1 | async-start | bytes 4194304 | tf_op jit(solution)/shard_map/all_to_all | solution.py:129
  140.4 19.3 %copy-start.8 = (bf16[4,2,128,1024]{3,2,1,0:T(8,128)(2,1)}, bf16[4,2,128,1024]{3,2,1,0:T(8,128)(2,1)S(1)}, u32[]{:S(2)}) copy-start(bf16[4,2,128,1024]{3,2,1,0:T(8,128)(2,1)S(1)} %all-to-all-done.1) | copy-start | bytes 6291460
  143.6 17.7 %all-to-all-start.2 = ((bf16[4,16,24,128]{3,2,1,0:T(8,128)(2,1)}), bf16[4,16,24,128]{3,2,1,0:T(8,128)(2,1)S(1)}, u32[]{:S(2)}, u32[]{:S(2)}) async-start(bf16[4,16,24,128]{3,2,1,0:T(8,128)(2,1)} %bitcast.122), calls=%async_computation.2 | async-start | bytes 786432 | tf_op jit(solution)/shard_map/all_to_all | solution.py:164
  161.3 71.6 %all-to-all-start.3 = ((bf16[4,16,24,128]{3,2,1,0:T(8,128)(2,1)}), bf16[4,16,24,128]{3,2,1,0:T(8,128)(2,1)S(1)}, u32[]{:S(2)}, u32[]{:S(2)}) async-start(bf16[4,16,24,128]{3,2,1,0:T(8,128)(2,1)} %bitcast.101), calls=%async_computation.3 | async-start | bytes 786432 | tf_op jit(solution)/shard_map/all_to_all | solution.py:164
  222.7 8.6 %copy-start.9 = (bf16[4,2,128,1024]{3,2,1,0:T(8,128)(2,1)S(1)}, bf16[4,2,128,1024]{3,2,1,0:T(8,128)(2,1)}, u32[]{:S(2)}) copy-start(bf16[4,2,128,1024]{3,2,1,0:T(8,128)(2,1)} %copy-done.8) | copy-start | bytes 6291460
  232.9 36.6 %all-to-all-start.4 = ((bf16[4,16,24,128]{3,2,1,0:T(8,128)(2,1)}), bf16[4,16,24,128]{3,2,1,0:T(8,128)(2,1)S(1)}, u32[]{:S(2)}, u32[]{:S(2)}) async-start(bf16[4,16,24,128]{3,2,1,0:T(8,128)(2,1)} %bitcast.100), calls=%async_computation.4 | async-start | bytes 786432 | tf_op jit(solution)/shard_map/all_to_all | solution.py:164
  243.7 7.5 %copy-start.12 = (bf16[3,48,1024]{2,0,1:T(4,128)(2,1)S(1)}, bf16[3,48,1024]{2,0,1:T(4,128)(2,1)}, u32[]{:S(2)}) copy-start(bf16[3,48,1024]{2,0,1:T(4,128)(2,1)} %copy.65) | copy-start | bytes 884740
  243.7 8.5 %copy-start.18 = (s32[48]{0:T(128)S(1)}, s32[48]{0:T(128)}, u32[]{:S(2)}) copy-start(s32[48]{0:T(128)} %param.20) | copy-start | bytes 580
  252.4 2.2 copy-start.2
  261.0 2.2 copy-start.4
  269.5 0.8 copy-start.6
  270.3 2.2 copy-start.3
  272.5 1.0 copy-start.5
  273.5 1.0 copy-start.7
  274.5 11.4 %copy-start.1 = (bf16[12,128,1024]{2,1,0:T(8,128)(2,1)S(1)}, bf16[12,128,1024]{2,1,0:T(8,128)(2,1)}, u32[]{:S(2)}) copy-start(bf16[12,128,1024]{2,1,0:T(8,128)(2,1)} %param.16) | copy-start | bytes 9437188
Sparse Core Ops, SparseCore 0:
  10.0 66.1 all-gather.3
  77.8 73.3 all-gather.5
  152.7 69.9 all-gather.7

commit v2 on v1

--- a/solution.py
+++ b/solution.py
@@ -18,7 +18,7 @@
     return (code_block.astype(jnp.float32) * scale_rows[..., None]).astype(jnp.bfloat16)
 
 
-def attend_kernel(n_steps, len_ref, q_ref, kv_ref, new_ref, out_ref):
+def attend_kernel(store, len_ref, q_ref, kv_ref, new_ref, *refs):
     inv_scale = HD ** (-0.5)
     ctx = kv_ref.shape[1]
     n_new = new_ref.shape[1]
@@ -50,17 +50,57 @@
         p_new = (e_new * inv).astype(jnp.bfloat16)
         out = lax.dot_general(p_old, kv_ref[:, :, v_cols], pv, preferred_element_type=jnp.float32)
         out += lax.dot_general(p_new, new_ref[:, :, v_cols], pv, preferred_element_type=jnp.float32)
-        out_ref[head] = out.astype(jnp.bfloat16)
-
-
-def attend(q, pages, fresh, row_lengths, n_steps):
+        store(refs[-1], head, out)
+
+
+def store_heads(out_ref, head, out):
+    out_ref[head] = out.astype(jnp.bfloat16)
+
+
+def store_columns(out_ref, head, out):
+    by_query = jnp.swapaxes(out, 0, 1).astype(jnp.bfloat16)
+    for step in range(out_ref.shape[0]):
+        for share in range(SHARE):
+            cols = pl.ds((head * SHARE + share) * HD, HD)
+            out_ref[step, :, cols] = by_query[step * SHARE + share]
+
+
+def attend_into(result, c, q, pages, fresh, row_lengths, row_dev):
+    _, rows, q_rows, _ = q.shape
+    ctx, kv_width = pages.shape[1:]
+    n_steps = q_rows // SHARE
+    lens = jnp.broadcast_to(row_lengths[:, None, None], (rows, 1, ctx))
+    earlier = [] if result is None else [result]
+    return pl.pallas_call(
+        functools.partial(attend_kernel, store_columns),
+        grid=(1,),
+        out_shape=jax.ShapeDtypeStruct((n_steps, row_dev, HEADS * HD), jnp.bfloat16),
+        in_specs=[
+            pl.BlockSpec((rows, 1, ctx), lambda i: (0, 0, 0)),
+            pl.BlockSpec(q.shape, lambda i: (0, 0, 0, 0)),
+            pl.BlockSpec(pages.shape, lambda i: (0, 0, 0)),
+            pl.BlockSpec(fresh.shape, lambda i: (0, 0, 0)),
+        ]
+        + [pl.BlockSpec(memory_space=pl.ANY)] * len(earlier),
+        out_specs=pl.BlockSpec((n_steps, rows, HEADS * HD), lambda i: (0, c, 0)),
+        input_output_aliases={4: 0} if earlier else {},
+        compiler_params=pltpu.CompilerParams(vmem_limit_bytes=40 * 1024 * 1024),
+        cost_estimate=pl.CostEstimate(
+            flops=4 * KVH * rows * q_rows * HD * ctx,
+            bytes_accessed=pages.size * 2 + 2 * q.size * 2,
+            transcendentals=KVH * rows * q_rows * ctx,
+        ),
+    )(lens, q, pages, fresh, *earlier)
+
+
+def attend(q, pages, fresh, row_lengths):
     _, rows, q_rows, _ = q.shape
     ctx, kv_width = pages.shape[1:]
     n_new = fresh.shape[1]
     block = 8 if rows % 8 == 0 else rows
     lens = jnp.broadcast_to(row_lengths[:, None, None], (rows, 1, ctx))
     return pl.pallas_call(
-        functools.partial(attend_kernel, n_steps),
+        functools.partial(attend_kernel, store_heads),
         grid=(rows // block,),
         out_shape=jax.ShapeDtypeStruct(q.shape, jnp.bfloat16),
         in_specs=[
@@ -77,6 +117,39 @@
             transcendentals=KVH * rows * q_rows * ctx,
         ),
     )(lens, q, pages, fresh)
+
+
+def block_dot(block, w_query, number):
+    depth = block.shape[1]
+    w_block = lax.dynamic_slice_in_dim(w_query, number * depth, depth, 0)
+    return jnp.dot(block, w_block, preferred_element_type=jnp.float32)
+
+
+def hop_once(from_left, from_right, hop, count):
+    right_pairs = [(i, i + 1) for i in range(hop - 1, count - 1)]
+    left_pairs = [(i + 1, i) for i in range(count - hop)]
+    return (
+        lax.ppermute(from_left, "tensor", right_pairs),
+        lax.ppermute(from_right, "tensor", left_pairs),
+    )
+
+
+def nth_block(arrived, k, count):
+    order = [
+        [(h, d) for h in range(1, count) for d in (-1, 1) if 0 <= i + d * h < count]
+        for i in range(count)
+    ]
+    me = lax.axis_index("tensor")
+    sources = sorted({order[i][k] for i in range(count)})
+    block = arrived[sources[0]]
+    number = me + sources[0][0] * sources[0][1]
+    for source in sources[1:]:
+        here = functools.reduce(
+            jnp.logical_or, [me == i for i in range(count) if order[i][k] == source]
+        )
+        block = jnp.where(here, arrived[source], block)
+        number = jnp.where(here, me + source[0] * source[1], number)
+    return block, number
 
 
 def on_device(
@@ -103,12 +176,11 @@
     row_chunk = row_dev // chunks
     group_index = lax.axis_index("dp")
 
-    by_dev = hidden.reshape(n_steps, n_tensor, row_dev, width_dev)
-    gathered = []
-    for c in range(chunks):
-        part = by_dev[:, :, c * row_chunk : (c + 1) * row_chunk]
-        part = part.reshape(n_steps * n_tensor * row_chunk, width_dev)
-        gathered.append(lax.all_gather(part, "tensor", axis=1, tiled=True))
+    flat = hidden.reshape(n_steps * n_rows, width_dev)
+    relay = 2 < n_tensor <= 8
+    arrived = {}
+    if relay:
+        arrived[(1, -1)], arrived[(1, 1)] = hop_once(flat, flat, 1, n_tensor)
 
     mine = variant_lists // owned == group_index
     rank_in = jnp.cumsum(mine.astype(jnp.int32), axis=1) - 1
@@ -125,6 +197,20 @@
         b_scales.at[picks].get(mode="promise_in_bounds"),
     ).reshape(n_dp, SLOTS, rank_size, col_count)
     n_slots = n_dp * SLOTS
+    pages = [
+        kv_cache.at[page_table[c * row_chunk : (c + 1) * row_chunk].reshape(-1)]
+        .get(mode="promise_in_bounds")
+        .reshape(row_chunk, -1, kv_cache.shape[2])
+        for c in range(chunks)
+    ]
+    total = None
+    if relay:
+        total = block_dot(flat, w_query, lax.axis_index("tensor"))
+        far_left, far_right, pages, total, _ = lax.optimization_barrier(
+            (arrived[(1, -1)], arrived[(1, 1)], pages, total, b_send)
+        )
+        arrived[(1, -1)], arrived[(1, 1)] = far_left, far_right
+        arrived[(2, -1)], arrived[(2, 1)] = hop_once(far_left, far_right, 2, n_tensor)
     a_select = lax.all_to_all(a_send, "dp", 0, 0, tiled=True).reshape(n_slots, width_dev, rank_size)
     b_select = lax.all_to_all(b_send, "dp", 0, 0, tiled=True).reshape(
         n_slots * rank_size, col_count
@@ -141,33 +227,58 @@
 
     low_all = jnp.einsum("trd,kdc->trkc", hidden, a_select, preferred_element_type=jnp.float32)
     low_part = jnp.sum(jnp.where(onehot[None, :, :, None], low_all, 0.0), axis=2)
-    low_bf = lax.psum(low_part, "tensor").astype(jnp.bfloat16)
+    if relay:
+        first, number = nth_block(arrived, 0, n_tensor)
+        total = total + block_dot(first, w_query, number)
+        far_left, far_right = arrived[(2, -1)], arrived[(2, 1)]
+        far_left, far_right, total, low_part = lax.optimization_barrier(
+            (far_left, far_right, total, low_part)
+        )
+        arrived[(2, -1)], arrived[(2, 1)] = far_left, far_right
+        for hop in range(3, n_tensor):
+            far_left, far_right = hop_once(far_left, far_right, hop, n_tensor)
+            arrived[(hop, -1)], arrived[(hop, 1)] = far_left, far_right
+    low_split = low_part.reshape(n_tensor, -1, rank_size)
+    low_mine = jnp.sum(lax.all_to_all(low_split, "tensor", 0, 0), axis=0).astype(jnp.bfloat16)
+    low_bf = lax.all_gather(low_mine, "tensor", axis=0, tiled=True)
+    low_bf = low_bf.reshape(n_steps, n_rows, rank_size)
     spread = jnp.where(onehot[None, :, :, None], low_bf[:, :, None, :], jnp.zeros((), jnp.bfloat16))
     spread = spread.reshape(n_steps, n_tensor, row_dev, n_slots * rank_size)
 
+    delta = jnp.dot(
+        spread.reshape(-1, n_slots * rank_size), b_select, preferred_element_type=jnp.float32
+    )
+    if relay:
+        for k in range(1, n_tensor - 2):
+            block, number = nth_block(arrived, k, n_tensor)
+            total = total + block_dot(block, w_query, number)
+        total = total + delta
+        last, last_number = nth_block(arrived, n_tensor - 2, n_tensor)
+    else:
+        total, last, last_number = delta, lax.all_gather(flat, "tensor", axis=1, tiled=True), 0
+    total = total.reshape(n_steps, n_tensor, row_dev, col_count)
+    last = last.reshape(n_steps, n_tensor, row_dev, -1)
+
     fresh = jnp.pad(new_kv.transpose(1, 0, 2), ((0, 0), (0, 16 - n_steps), (0, 0)))
     head_dev = col_count // HD
-    outs = []
+    outs, result = [], None
     for c in range(chunks):
         rows = slice(c * row_chunk, (c + 1) * row_chunk)
-        pages = kv_cache.at[page_table[rows].reshape(-1)].get(mode="promise_in_bounds")
-        pages = pages.reshape(row_chunk, -1, kv_cache.shape[2])
-        base = jnp.dot(gathered[c], w_query, preferred_element_type=jnp.float32)
-        delta = jnp.dot(
-            spread[:, :, rows].reshape(-1, n_slots * rank_size),
-            b_select,
-            preferred_element_type=jnp.float32,
-        )
-        q = (base + delta).astype(jnp.bfloat16)
+        part = last[:, :, rows].reshape(-1, last.shape[3])
+        q = block_dot(part, w_query, last_number) + total[:, :, rows].reshape(-1, col_count)
+        q = q.astype(jnp.bfloat16)
         q = q.reshape(n_steps, n_tensor, row_chunk, head_dev, HD).transpose(1, 2, 0, 3, 4)
         q = q.reshape(n_tensor, row_chunk, n_steps * head_dev, HD)
         q = lax.all_to_all(q, "tensor", 0, 0, tiled=True)
         q = q.reshape(KVH, n_tensor // KVH, row_chunk, n_steps, head_dev, HD)
         q = q.transpose(0, 2, 3, 1, 4, 5).reshape(KVH, row_chunk, n_steps * SHARE, HD)
-        out = attend(q, pages, fresh[rows], lengths[rows], n_steps)
-        out = out.reshape(KVH, row_chunk, n_steps, SHARE * HD).transpose(2, 1, 0, 3)
-        outs.append(out.reshape(n_steps, row_chunk, HEADS * HD))
-    return jnp.concatenate(outs, axis=1)
+        if row_chunk % 16 == 0:
+            result = attend_into(result, c, q, pages[c], fresh[rows], lengths[rows], row_dev)
+        else:
+            out = attend(q, pages[c], fresh[rows], lengths[rows])
+            out = out.reshape(KVH, row_chunk, n_steps, SHARE * HD).transpose(2, 1, 0, 3)
+            outs.append(out.reshape(n_steps, row_chunk, HEADS * HD))
+    return jnp.concatenate(outs, axis=1) if outs else result
 
 
 def solution(mesh):

time: 293 us -> 270 us (0.922)
  waiting for transfers between devices: 95.5 us -> 55.4 us
  blocking collectives: 36.2 us -> 64.9 us
  starting transfers between devices: 19.3 us -> 37 us
  local copies, waits for them, and re-layouts: 63.6 us -> 47.8 us
  between operations: 13.5 us -> 0.41 us
    all_gather x3 -> x0, waiting for transfers between devices: 61.9 us -> none  [on_device(): gathered.append(lax.all_gather(part, 'tensor', axis=1, tiled=True))]
    all_gather x0 -> x1, blocking collectives: none -> 52.9 us  [on_device(): low_bf = lax.all_gather(low_mine, 'tensor', axis=0, tiled=True)]
    ppermute x0 -> x6, waiting for transfers between devices: none -> 39.3 us  [the longest x3 39.3 us: hop_once(): lax.ppermute(from_right, 'tensor', left_pairs)]
    psum x1 -> x0, blocking collectives: 36.2 us -> none  [on_device(): low_bf = lax.psum(low_part, 'tensor').astype(jnp.bfloat16)]
    all_to_all x1, waiting for transfers between devices: 32.2 us -> 5.6 us  [on_device(): lax.all_to_all(a_send, 'dp', 0, 0, tiled=True)]
    ppermute x0 -> x6, starting transfers between devices: none -> 15.4 us  [the longest x3 11.3 us: hop_once(): lax.ppermute(from_left, 'tensor', right_pairs)]
    all_to_all x0 -> x1, blocking collectives: none -> 12 us  [on_device(): lax.all_to_all(low_split, 'tensor', 0, 0)]
    all_to_all x3, waiting for transfers between devices: 0.01 us -> 10.4 us  [on_device(): q = lax.all_to_all(q, 'tensor', 0, 0, tiled=True)]
  transfers between devices with their start and end apart: 8 -> 11, of which waited for: 3 -> 4; matrix products, arithmetic and copies ran while one was open for 32% -> 31% of each run, Pallas kernels for 3% -> 3%
where the time goes in v2:
time: 270 us; the launch traced here: 269 us
  blocking collectives  64.9 us (24%)
  waiting for transfers between devices  55.4 us (21%)
  local copies, waits for them, and re-layouts  47.8 us (18%)
  starting transfers between devices  37 us (14%)
  matrix products  35.8 us (13%)
  other arithmetic  15 us (6%)
  Pallas kernels  12.4 us (5%)
    all_gather x1, blocking collectives, on_device(): low_bf = lax.all_gather(low_mine, 'tensor', axis=0, tiled=True)  52.9 us
    ppermute x3, waiting for transfers between devices, hop_once(): lax.ppermute(from_right, 'tensor', left_pairs)  39.3 us
    dot_general x6, matrix products, block_dot(): return jnp.dot(block, w_block, preferred_element_type=jnp.float32)  26.8 us
    gather x3, local copies, waits for them, and re-layouts, on_device(): pages = [kv_cache.at[page_table[c * row_chunk:(c + 1) * row_chunk].reshap...  22.3 us
    pallas_call x3, Pallas kernels, attend_into(): pl.pallas_call(functools.partial(attend_kernel, store_columns), grid=(1,)...  12.4 us
    all_to_all x3, starting transfers between devices, on_device(): q = lax.all_to_all(q, 'tensor', 0, 0, tiled=True)  12.1 us
    all_to_all x1, blocking collectives, on_device(): lax.all_to_all(low_split, 'tensor', 0, 0)  12 us
    ppermute x3, starting transfers between devices, hop_once(): lax.ppermute(from_left, 'tensor', right_pairs)  11.3 us
  transfers between devices with their start and end apart: 11, of which 4 were waited for; matrix products, arithmetic and copies ran while one was open for 31% of the time, Pallas kernels for 3%

profile of v2, /device:TPU:0, one launch (start us, length us, event | category | flops | bytes accessed | tf_op | source)
XLA Modules:
  0.0 268.7 jit_solution(17783589753073006269)
XLA Ops:
  0.0 1.5 collective-permute-start.1
  1.6 7.0 %collective-permute-start = (bf16[576,2048]{1,0:T(8,128)(2,1)}, bf16[576,2048]{1,0:T(8,128)(2,1)}, u32[]{:S(2)}, u32[]{:S(2)}) collective-permute-start(bf16[576,2048]{1,0:T(8,128)(2,1)} %bitcast.119), channel_id=1, source_target_pairs={{0,1},{1,2},{2,3},{4,5},{5,6},{6,7},{8,9},{9,10},{10,11},{12,13},{... | collective-permute-start | bytes 7077896 | tf_op jit(solution)/shard_map/ppermute | solution.py:132
  8.6 0.7 fusion.73
  9.3 0.2 reduce_window_sum.11
  9.5 0.7 add_select_fusion
  10.2 0.1 select_reduce_fusion.2
  10.3 0.1 copy.33
  10.4 0.1 reshape.290
  10.5 1.5 gather_fusion.6
  12.1 5.8 %gather_fusion.5 = bf16[8,2048,128]{2,1,0:T(8,128)(2,1)} fusion(bf16[12,2048,128]{2,1,0:T(8,128)(2,1)} %param.14, s32[1024]{0:T(1024)S(1)} %pad_clamp_fusion), kind=kCustom, calls=%fused_computation.5 | custom fusion | bytes 8388640 | tf_op jit(solution)/shard_map/gather | solution.py:192
  17.9 5.8 %fusion = bf16[4,2,2048,128]{3,2,1,0:T(8,128)(2,1)} fusion(bf16[4,2,2048,128]{3,2,1,0:T(8,128)(2,1)} %bitcast.100, f32[4,2,2048]{2,1,0:T(2,128)S(1)} %mul.50), kind=kLoop, calls=%fused_computation.8 | loop fusion | flops 6291456 | bytes 8454144 | tf_op jit(solution)/shard_map/convert_element_type | solution.py:18
  23.7 5.0 %all-to-all-start = ((bf16[4,2,2048,128]{3,2,1,0:T(8,128)(2,1)}), bf16[4,2,2048,128]{3,2,1,0:T(8,128)(2,1)}, u32[]{:S(2)}, u32[]{:S(2)}) async-start(bf16[4,2,2048,128]{3,2,1,0:T(8,128)(2,1)} %fusion), calls=%async_computation | async-start | bytes 8388608 | tf_op jit(solution)/shard_map/all_to_all | solution.py:214
  28.7 0.6 gather_fusion.4
  29.4 0.1 reshape.288
  29.6 0.1 reshape.284
  29.8 0.1 reshape.286
  29.9 2.0 gather_fusion.3
  31.9 7.4 %gather_fusion.1 = bf16[128,16,1024]{2,1,0:T(8,128)(2,1)} fusion(bf16[384,16,1024]{2,1,0:T(8,128)(2,1)} %param.23, s32[1024]{0:T(1024)S(1)} %pad_clamp_fusion.2), kind=kCustom, calls=%fused_computation.1 | custom fusion | bytes 8389120 | tf_op jit(solution)/shard_map/gather | solution.py:202
  39.3 7.4 %gather_fusion = bf16[128,16,1024]{2,1,0:T(8,128)(2,1)} fusion(bf16[384,16,1024]{2,1,0:T(8,128)(2,1)} %param.23, s32[1024]{0:T(1024)S(1)} %pad_clamp_fusion.3), kind=kCustom, calls=%fused_computation | custom fusion | bytes 8389120 | tf_op jit(solution)/shard_map/gather | solution.py:202
  46.7 7.5 %gather_fusion.2 = bf16[128,16,1024]{2,1,0:T(8,128)(2,1)} fusion(bf16[384,16,1024]{2,1,0:T(8,128)(2,1)} %param.23, s32[1024]{0:T(1024)S(1)} %pad_clamp_fusion.1), kind=kCustom, calls=%fused_computation.2 | custom fusion | bytes 8389120 | tf_op jit(solution)/shard_map/gather | solution.py:202
  54.2 1.7 fusion.1
  55.9 0.6 copy-done.16
  56.5 4.4 %fusion.23 = f32[576,1024]{1,0:T(8,128)S(1)} fusion(bf16[576,2048]{1,0:T(8,128)(2,1)S(1)} %bitcast.120, bf16[8192,1024]{1,0:T(8,128)(2,1)} %param.13, s32[]{:T(128)S(6)} %select_n.170), kind=kOutput, calls=%fused_computation.38 | convolution fusion | flops 2415919104 | bytes 8912900 | tf_op jit(solution)/shard_map/dot_general | solution.py:125
  61.0 2.2 collective-permute-start.2
  63.2 1.3 collective-permute-start.3
  64.5 0.7 bitcast_select_fusion.1
  65.2 0.2 select_reduce_fusion.1
  65.5 5.1 %fusion.4 = f32[576,1024]{1,0:T(8,128)S(1)} fusion(bf16[8192,1024]{1,0:T(8,128)(2,1)} %param.13, s32[]{:T(128)S(6)} %select_n.177, bf16[576,2048]{1,0:T(8,128)(2,1)} %collective-permute-done.1, bf16[576,2048]{1,0:T(8,128)(2,1)} %collective-permute-done, pred[]{:T(512)S(6)} %eq.78), kind=kOutput, calls=%fused_computation.13 | convolution fusion | flops 2417098752 | bytes 11272197 | tf_op jit(solution)/shard_map/dot_general | solution.py:125
  70.7 0.7 add.141
  71.3 5.6 %all-to-all-done = bf16[4,2,2048,128]{3,2,1,0:T(8,128)(2,1)} async-done(((bf16[4,2,2048,128]{3,2,1,0:T(8,128)(2,1)}), bf16[4,2,2048,128]{3,2,1,0:T(8,128)(2,1)}, u32[]{:S(2)}, u32[]{:S(2)}) %all-to-all-start) | async-done | bytes 4194336 | tf_op jit(solution)/shard_map/all_to_all | solution.py:214
  76.9 5.6 %fusion.14 = f32[3,192,128]{2,1,0:T(8,128)S(1)} fusion(pred[192,8]{0,1:T(8,128)(4,1)S(1)} %iota_compare_fusion, bf16[8,2048,128,1]{2,1,3,0:T(8,128)(2,1)} %bitcast.19, bf16[3,192,2048]{2,1,0:T(8,128)(2,1)} %param.12), kind=kOutput, calls=%fused_computation.27 | convolution fusion | flops 2417025024 | bytes 6850048 | tf_op jit(solution)/shard_map/trd,kdc->trkc/dot_general | solution.py:228
  82.5 39.3 %collective-permute-done.3 = bf16[576,2048]{1,0:T(8,128)(2,1)} collective-permute-done((bf16[576,2048]{1,0:T(8,128)(2,1)}, bf16[576,2048]{1,0:T(8,128)(2,1)}, u32[]{:S(2)}, u32[]{:S(2)}) %collective-permute-start.3) | collective-permute-done | bytes 2359328 | tf_op jit(solution)/shard_map/ppermute | solution.py:133
  121.8 12.0 %all_to_all.30 = f32[4,144,128]{2,1,0:T(8,128)S(1)} all-to-all(f32[4,144,128]{2,1,0:T(8,128)S(1)} %bitcast.116), channel_id=1, replica_groups=mesh['replica'=2,'dp'=4,'tensor'=4] {'tensor'}, dimensions={0} | all-to-all | bytes 589824 | tf_op jit(solution)/shard_map/all_to_all | solution.py:242
  133.8 4.5 %all-to-all-start.2 = ((bf16[4,2,128,1024]{3,2,1,0:T(8,128)(2,1)}), bf16[4,2,128,1024]{3,2,1,0:T(8,128)(2,1)}, u32[]{:S(2)}, u32[]{:S(2)}) async-start(bf16[4,2,128,1024]{3,2,1,0:T(8,128)(2,1)} %fusion.1), calls=%async_computation.2 | async-start | bytes 4194304 | tf_op jit(solution)/shard_map/all_to_all | solution.py:215
  138.3 1.3 collective-permute-start.4
  139.6 2.1 collective-permute-start.5
  141.7 7.6 %fusion.2 = f32[576,1024]{1,0:T(8,128)} fusion(bf16[8192,1024]{1,0:T(8,128)(2,1)} %param.13, s32[]{:T(128)S(6)} %select_n.197, bf16[576,2048]{1,0:T(8,128)(2,1)} %collective-permute-done.3, bf16[576,2048]{1,0:T(8,128)(2,1)} %collective-permute-done.2, bf16[576,2048]{1,0:T(8,128)(2,1)} %collective-permute-done.1, pred[]{:T(512)S(6)} %eq.94, pred[]{:T(512)S(6)} %eq.78), kind=kOutput, calls=%fused_computation.11 | convolution fusion | flops 2418278400 | bytes 13631494 | tf_op jit(solution)/shard_map/dot_general | solution.py:125
  149.3 52.9 %all_gather.3 = bf16[576,128]{1,0:T(8,128)(2,1)S(1)} all-gather(bf16[144,128]{1,0:T(8,128)(2,1)S(1)} %reduce_sum.52), channel_id=1, replica_groups=mesh['replica'=2,'dp'=4,'tensor'=4] {'tensor'}, dimensions={0}, use_global_device_ids=true | all-gather | bytes 184320 | tf_op jit(solution)/shard_map/all_gather | solution.py:243
  202.2 0.3 broadcast_select_fusion
  202.5 1.8 copy.34
  204.3 3.5 %fusion.53 = f32[576,1024]{1,0:T(8,128)S(1)} fusion(bf16[1024,1024]{1,0:T(8,128)(2,1)} %bitcast.26, bf16[72,8,8,128]{3,2,1,0:T(8,128)(2,1)} %bitcast.114), kind=kOutput, calls=%fused_computation.48 | convolution fusion | flops 1207959552 | bytes 5636096 | tf_op jit(solution)/shard_map/dot_general | solution.py:248
  207.8 1.0 add_add_fusion
  208.8 1.1 fusion.76
  209.9 2.8 %select_select_fusion = bf16[576,2048]{1,0:T(8,128)(2,1)S(1)} fusion(bf16[576,2048]{1,0:T(8,128)(2,1)} %collective-permute-done.4, bf16[576,2048]{1,0:T(8,128)(2,1)} %collective-permute-done.5, bf16[576,2048]{1,0:T(8,128)(2,1)} %collective-permute-done.3, bf16[576,2048]{1,0:T(8,128)(2,1)} %collective-permute-done.2, pred[]{:T(512)S(6)} %eq.95, pred[]{:T(512)S(6)} %eq.94, ...), kind=kLoop, calls=%fused_computation.33 | loop fusion | flops 3538944 | bytes 11796483 | tf_op jit(solution)/shard_map/jit(_where)/select_n | solution.py:150
  212.7 1.4 fusion.75
  214.2 3.2 %fusion.47 = bf16[24,8,8,128]{3,1,2,0:T(8,128)(2,1)S(1)} fusion(f32[192,1024]{1,0:T(8,128)S(1)} %bitcast.107, bf16[192,2048]{1,0:T(8,128)(2,1)S(1)} %bitcast.109, bf16[8192,1024]{1,0:T(8,128)(2,1)} %param.13, s32[]{:T(128)S(6)} %select_n.192), kind=kOutput, calls=%fused_computation.46 | convolution fusion | flops 805699584 | bytes 6160388 | tf_op jit(solution)/shard_map/dot_general | solution.py:125
  217.5 0.8 copy.53
  218.3 5.0 %all-to-all-start.4 = ((bf16[4,16,24,128]{3,2,1,0:T(8,128)(2,1)}), bf16[4,16,24,128]{3,2,1,0:T(8,128)(2,1)S(1)}, u32[]{:S(2)}, u32[]{:S(2)}) async-start(bf16[4,16,24,128]{3,2,1,0:T(8,128)(2,1)} %bitcast.94), calls=%async_computation.4 | async-start | bytes 786432 | tf_op jit(solution)/shard_map/all_to_all | solution.py:272
  223.3 3.2 %fusion.50 = bf16[24,8,8,128]{3,1,2,0:T(8,128)(2,1)S(1)} fusion(f32[192,1024]{1,0:T(8,128)S(1)} %bitcast.105, bf16[192,2048]{1,0:T(8,128)(2,1)S(1)} %bitcast.108, bf16[8192,1024]{1,0:T(8,128)(2,1)} %param.13, s32[]{:T(128)S(6)} %select_n.192), kind=kOutput, calls=%fused_computation.47 | convolution fusion | flops 805699584 | bytes 6160388 | tf_op jit(solution)/shard_map/dot_general | solution.py:125
  226.5 0.8 copy.52
  227.3 5.3 %all-to-all-done.4.q_ref = bf16[4,16,24,128]{3,2,1,0:T(8,128)(2,1)S(1)} async-done(((bf16[4,16,24,128]{3,2,1,0:T(8,128)(2,1)}), bf16[4,16,24,128]{3,2,1,0:T(8,128)(2,1)S(1)}, u32[]{:S(2)}, u32[]{:S(2)}) %all-to-all-start.4) | async-done | bytes 393248 | tf_op jit(solution)/shard_map/all_to_all | solution.py:272
  232.6 3.5 %all-to-all-start.5 = ((bf16[4,16,24,128]{3,2,1,0:T(8,128)(2,1)}), bf16[4,16,24,128]{3,2,1,0:T(8,128)(2,1)S(1)}, u32[]{:S(2)}, u32[]{:S(2)}) async-start(bf16[4,16,24,128]{3,2,1,0:T(8,128)(2,1)} %bitcast.93), calls=%async_computation.5 | async-start | bytes 786432 | tf_op jit(solution)/shard_map/all_to_all | solution.py:272
  236.1 3.2 %fusion.44 = bf16[24,8,8,128]{3,1,2,0:T(8,128)(2,1)S(1)} fusion(f32[192,1024]{1,0:T(8,128)S(1)} %bitcast.104, bf16[192,2048]{1,0:T(8,128)(2,1)S(1)} %bitcast.106, bf16[8192,1024]{1,0:T(8,128)(2,1)} %param.13, s32[]{:T(128)S(6)} %select_n.192), kind=kOutput, calls=%fused_computation.45 | convolution fusion | flops 805699584 | bytes 6160388 | tf_op jit(solution)/shard_map/dot_general | solution.py:125
  239.4 0.8 copy.55
  240.2 5.1 %all-to-all-done.5.q_ref = bf16[4,16,24,128]{3,2,1,0:T(8,128)(2,1)S(1)} async-done(((bf16[4,16,24,128]{3,2,1,0:T(8,128)(2,1)}), bf16[4,16,24,128]{3,2,1,0:T(8,128)(2,1)S(1)}, u32[]{:S(2)}, u32[]{:S(2)}) %all-to-all-start.5) | async-done | bytes 393248 | tf_op jit(solution)/shard_map/all_to_all | solution.py:272
  245.4 3.7 %all-to-all-start.3 = ((bf16[4,16,24,128]{3,2,1,0:T(8,128)(2,1)}), bf16[4,16,24,128]{3,2,1,0:T(8,128)(2,1)S(1)}, u32[]{:S(2)}, u32[]{:S(2)}) async-start(bf16[4,16,24,128]{3,2,1,0:T(8,128)(2,1)} %bitcast.96), calls=%async_computation.3 | async-start | bytes 786432 | tf_op jit(solution)/shard_map/all_to_all | solution.py:272
  249.1 0.3 copy.54
  249.3 1.1 pad_slice_fusion
  250.6 2.2 copy-done.4
  252.8 4.1 %shard_map.118.refs_0_ = bf16[3,48,4096]{2,1,0:T(8,128)(2,1)} custom-call(s32[16,1,128]{2,1,0:T(1,128)S(1)} %broadcast_in_dim.119.len_ref, bf16[4,16,24,128]{3,2,1,0:T(8,128)(2,1)S(1)} %all-to-all-done.5.q_ref, bf16[16,128,1024]{2,1,0:T(8,128)(2,1)S(1)} %bitcast.99, bf16[16,16,1024]{2,1,0:T(8,128)(2,1)S(1)} %get-tuple-element.36.new_ref), custom_call_target="tpu_custom_call" | custom-call | flops 100663296 | bytes 4980736 | tf_op jit(solution)/shard_map/pallas_call | solution.py:74
  257.0 4.1 %shard_map.119.refs_0_ = bf16[3,48,4096]{2,1,0:T(8,128)(2,1)} custom-call(s32[16,1,128]{2,1,0:T(1,128)S(1)} %broadcast_in_dim.118.len_ref, bf16[4,16,24,128]{3,2,1,0:T(8,128)(2,1)S(1)} %all-to-all-done.4.q_ref, bf16[16,128,1024]{2,1,0:T(8,128)(2,1)S(1)} %bitcast.98, ...), custom_call_target="tpu_custom_call", output_to_operand_aliasing={{}: (4, {})} | custom-call | flops 100663296 | bytes 4980736 | tf_op jit(solution)/shard_map/pallas_call | solution.py:74
  261.2 2.3 copy-done.2
  263.5 1.0 copy-done.5
  264.6 4.1 %shard_map.120 = bf16[3,48,4096]{2,1,0:T(8,128)(2,1)} custom-call(s32[16,1,128]{2,1,0:T(1,128)S(1)} %broadcast_in_dim.70.len_ref, bf16[4,16,24,128]{3,2,1,0:T(8,128)(2,1)S(1)} %all-to-all-done.3.q_ref, bf16[16,128,1024]{2,1,0:T(8,128)(2,1)S(1)} %bitcast.97, bf16[16,16,1024]{2,1,0:T(8,128)(2,1)S(1)} %copy-done.5, ...), custom_call_target="tpu_custom_call", output_to_operand_aliasing={{}: (4, {})} | custom-call | flops 100663296 | bytes 4980736 | tf_op jit(solution)/shard_map/pallas_call | solution.py:74
  (61 shorter events, 1.1 us)
Async XLA Ops:
  0.0 29.9 %copy-start = (bf16[12,128,1024]{2,1,0:T(8,128)(2,1)S(1)}, bf16[12,128,1024]{2,1,0:T(8,128)(2,1)}, u32[]{:S(2)}) copy-start(bf16[12,128,1024]{2,1,0:T(8,128)(2,1)} %param.16) | copy-start | bytes 9437188
  0.0 61.0 %collective-permute-start.1 = (bf16[576,2048]{1,0:T(8,128)(2,1)}, bf16[576,2048]{1,0:T(8,128)(2,1)}, u32[]{:S(2)}, u32[]{:S(2)}) collective-permute-start(bf16[576,2048]{1,0:T(8,128)(2,1)} %bitcast.118), channel_id=1, source_target_pairs={{1,0},{2,1},{3,2},{5,4},{6,5},{7,6},{9,8},{10,9},{11,10},{13,12},{... | collective-permute-start | bytes 7077896 | tf_op jit(solution)/shard_map/ppermute | solution.py:133
  1.6 59.4 %collective-permute-start = (bf16[576,2048]{1,0:T(8,128)(2,1)}, bf16[576,2048]{1,0:T(8,128)(2,1)}, u32[]{:S(2)}, u32[]{:S(2)}) collective-permute-start(bf16[576,2048]{1,0:T(8,128)(2,1)} %bitcast.119), channel_id=1, source_target_pairs={{0,1},{1,2},{2,3},{4,5},{5,6},{6,7},{8,9},{9,10},{10,11},{12,13},{... | collective-permute-start | bytes 7077896 | tf_op jit(solution)/shard_map/ppermute | solution.py:132
  23.7 5.0 %copy-start.12 = (f32[12,128]{1,0:T(8,128)S(1)}, f32[12,128]{1,0:T(8,128)}, u32[]{:S(2)}) copy-start(f32[12,128]{1,0:T(8,128)} %param.17) | copy-start | bytes 18436
  23.7 5.6 %copy-start.13 = (s32[48,8]{0,1:T(8,128)S(1)}, s32[48,8]{0,1:T(8,128)}, u32[]{:S(2)}) copy-start(s32[48,8]{0,1:T(8,128)} %param.21) | copy-start | bytes 4612
  23.7 53.2 %all-to-all-start = ((bf16[4,2,2048,128]{3,2,1,0:T(8,128)(2,1)}), bf16[4,2,2048,128]{3,2,1,0:T(8,128)(2,1)}, u32[]{:S(2)}, u32[]{:S(2)}) async-start(bf16[4,2,2048,128]{3,2,1,0:T(8,128)(2,1)} %fusion), calls=%async_computation | async-start | bytes 8388608 | tf_op jit(solution)/shard_map/all_to_all | solution.py:214
  46.7 7.5 %copy-start.6 = (bf16[8,128,1024]{2,1,0:T(8,128)(2,1)S(1)}, bf16[8,128,1024]{2,1,0:T(8,128)(2,1)}, u32[]{:S(2)}) copy-start(bf16[8,128,1024]{2,1,0:T(8,128)(2,1)} %gather_fusion.3) | copy-start | bytes 6291460
  54.2 2.4 copy-start.16
  56.5 8.9 %copy-start.15 = (s32[192]{0:T(256)S(1)}, s32[192]{0:T(256)}, u32[]{:S(2)}) copy-start(s32[192]{0:T(256)} %param.19) | copy-start | bytes 2308
  61.0 21.5 %collective-permute-start.2 = (bf16[576,2048]{1,0:T(8,128)(2,1)}, bf16[576,2048]{1,0:T(8,128)(2,1)}, u32[]{:S(2)}, u32[]{:S(2)}) collective-permute-start(bf16[576,2048]{1,0:T(8,128)(2,1)} %collective-permute-done), channel_id=1, source_target_pairs={{1,2},{2,3},{5,6},{6,7},{9,10},{10,11},{13,14},{14,15},{17,18},{18... | collective-permute-start | bytes 7077896 | tf_op jit(solution)/shard_map/ppermute | solution.py:132
  63.2 58.6 %collective-permute-start.3 = (bf16[576,2048]{1,0:T(8,128)(2,1)}, bf16[576,2048]{1,0:T(8,128)(2,1)}, u32[]{:S(2)}, u32[]{:S(2)}) collective-permute-start(bf16[576,2048]{1,0:T(8,128)(2,1)} %collective-permute-done.1), channel_id=1, source_target_pairs={{1,0},{2,1},{5,4},{6,5},{9,8},{10,9},{13,12},{14,13},{17,16},{18,1... | collective-permute-start | bytes 7077896 | tf_op jit(solution)/shard_map/ppermute | solution.py:133
  133.8 70.5 %all-to-all-start.2 = ((bf16[4,2,128,1024]{3,2,1,0:T(8,128)(2,1)}), bf16[4,2,128,1024]{3,2,1,0:T(8,128)(2,1)}, u32[]{:S(2)}, u32[]{:S(2)}) async-start(bf16[4,2,128,1024]{3,2,1,0:T(8,128)(2,1)} %fusion.1), calls=%async_computation.2 | async-start | bytes 4194304 | tf_op jit(solution)/shard_map/all_to_all | solution.py:215
  138.3 71.6 %collective-permute-start.4 = (bf16[576,2048]{1,0:T(8,128)(2,1)}, bf16[576,2048]{1,0:T(8,128)(2,1)}, u32[]{:S(2)}, u32[]{:S(2)}) collective-permute-start(bf16[576,2048]{1,0:T(8,128)(2,1)} %collective-permute-done.3), channel_id=1, source_target_pairs={{1,0},{5,4},{9,8},{13,12},{17,16},{21,20},{25,24},{29,28}} | collective-permute-start | bytes 7077896 | tf_op jit(solution)/shard_map/ppermute | solution.py:133
  139.6 70.3 %collective-permute-start.5 = (bf16[576,2048]{1,0:T(8,128)(2,1)}, bf16[576,2048]{1,0:T(8,128)(2,1)}, u32[]{:S(2)}, u32[]{:S(2)}) collective-permute-start(bf16[576,2048]{1,0:T(8,128)(2,1)} %collective-permute-done.2), channel_id=1, source_target_pairs={{2,3},{6,7},{10,11},{14,15},{18,19},{22,23},{26,27},{30,31}} | collective-permute-start | bytes 7077896 | tf_op jit(solution)/shard_map/ppermute | solution.py:132
  204.3 3.5 %copy-start.10 = (f32[576,1024]{1,0:T(8,128)S(1)}, f32[576,1024]{1,0:T(8,128)}, u32[]{:S(2)}) copy-start(f32[576,1024]{1,0:T(8,128)} %fusion.2) | copy-start | bytes 7077892
  217.4 5.9 %copy-start.7 = (f32[3,4,16,1024]{3,2,1,0:T(8,128)S(1)}, f32[3,4,16,1024]{3,2,1,0:T(8,128)}, u32[]{:S(2)}) copy-start(f32[3,4,16,1024]{3,2,1,0:T(8,128)} %get-tuple-element.33) | copy-start | bytes 2359300
  217.4 5.9 %copy-start.9 = (bf16[3,4,16,2048]{3,2,1,0:T(8,128)(2,1)S(1)}, bf16[3,4,16,2048]{3,2,1,0:T(8,128)(2,1)}, u32[]{:S(2)}) copy-start(bf16[3,4,16,2048]{3,2,1,0:T(8,128)(2,1)} %get-tuple-element.30) | copy-start | bytes 2359300
  218.3 14.3 %all-to-all-start.4 = ((bf16[4,16,24,128]{3,2,1,0:T(8,128)(2,1)}), bf16[4,16,24,128]{3,2,1,0:T(8,128)(2,1)S(1)}, u32[]{:S(2)}, u32[]{:S(2)}) async-start(bf16[4,16,24,128]{3,2,1,0:T(8,128)(2,1)} %bitcast.94), calls=%async_computation.4 | async-start | bytes 786432 | tf_op jit(solution)/shard_map/all_to_all | solution.py:272
  226.4 9.7 %copy-start.8 = (bf16[3,4,16,2048]{3,2,1,0:T(8,128)(2,1)S(1)}, bf16[3,4,16,2048]{3,2,1,0:T(8,128)(2,1)}, u32[]{:S(2)}) copy-start(bf16[3,4,16,2048]{3,2,1,0:T(8,128)(2,1)} %get-tuple-element.32) | copy-start | bytes 2359300
  232.6 12.7 %all-to-all-start.5 = ((bf16[4,16,24,128]{3,2,1,0:T(8,128)(2,1)}), bf16[4,16,24,128]{3,2,1,0:T(8,128)(2,1)S(1)}, u32[]{:S(2)}, u32[]{:S(2)}) async-start(bf16[4,16,24,128]{3,2,1,0:T(8,128)(2,1)} %bitcast.93), calls=%async_computation.5 | async-start | bytes 786432 | tf_op jit(solution)/shard_map/all_to_all | solution.py:272
  239.3 9.7 %copy-start.11 = (bf16[3,48,1024]{2,1,0:T(8,128)(2,1)S(1)}, bf16[3,48,1024]{2,1,0:T(8,128)(2,1)}, u32[]{:S(2)}) copy-start(bf16[3,48,1024]{2,1,0:T(8,128)(2,1)} %param.22) | copy-start | bytes 884740
  239.3 11.1 %copy-start.14 = (s32[48]{0:T(128)S(1)}, s32[48]{0:T(128)}, u32[]{:S(2)}) copy-start(s32[48]{0:T(128)} %param.20) | copy-start | bytes 580
  245.4 15.8 %all-to-all-start.3 = ((bf16[4,16,24,128]{3,2,1,0:T(8,128)(2,1)}), bf16[4,16,24,128]{3,2,1,0:T(8,128)(2,1)S(1)}, u32[]{:S(2)}, u32[]{:S(2)}) async-start(bf16[4,16,24,128]{3,2,1,0:T(8,128)(2,1)} %bitcast.96), calls=%async_computation.3 | async-start | bytes 786432 | tf_op jit(solution)/shard_map/all_to_all | solution.py:272
  250.6 2.2 copy-start.4
  252.8 4.2 %copy-start.3 = (bf16[128,16,1024]{2,1,0:T(8,128)(2,1)S(1)}, bf16[128,16,1024]{2,1,0:T(8,128)(2,1)}, u32[]{:S(2)}) copy-start(bf16[128,16,1024]{2,1,0:T(8,128)(2,1)} %gather_fusion.1) | copy-start | bytes 12582916
  261.2 7.5 %copy-start.1 = (bf16[12,128,1024]{2,1,0:T(8,128)(2,1)S(1)}, bf16[12,128,1024]{2,1,0:T(8,128)(2,1)}, u32[]{:S(2)}) copy-start(bf16[12,128,1024]{2,1,0:T(8,128)(2,1)} %param.16) | copy-start | bytes 9437188
  261.2 2.3 copy-start.2
  263.5 1.0 copy-start.5

commit v3 on v2

--- a/solution.py
+++ b/solution.py
@@ -65,24 +65,27 @@
             out_ref[step, :, cols] = by_query[step * SHARE + share]
 
 
-def attend_into(result, c, q, pages, fresh, row_lengths, row_dev):
+def attend_into(result, first_row, q, pages, fresh, row_lengths, row_dev):
     _, rows, q_rows, _ = q.shape
     ctx, kv_width = pages.shape[1:]
     n_steps = q_rows // SHARE
     lens = jnp.broadcast_to(row_lengths[:, None, None], (rows, 1, ctx))
     earlier = [] if result is None else [result]
+    block = 16
     return pl.pallas_call(
         functools.partial(attend_kernel, store_columns),
-        grid=(1,),
+        grid=(rows // block,),
         out_shape=jax.ShapeDtypeStruct((n_steps, row_dev, HEADS * HD), jnp.bfloat16),
         in_specs=[
-            pl.BlockSpec((rows, 1, ctx), lambda i: (0, 0, 0)),
-            pl.BlockSpec(q.shape, lambda i: (0, 0, 0, 0)),
-            pl.BlockSpec(pages.shape, lambda i: (0, 0, 0)),
-            pl.BlockSpec(fresh.shape, lambda i: (0, 0, 0)),
+            pl.BlockSpec((block, 1, ctx), lambda i: (i, 0, 0)),
+            pl.BlockSpec((KVH, block, q_rows, HD), lambda i: (0, i, 0, 0)),
+            pl.BlockSpec((block, ctx, kv_width), lambda i: (i, 0, 0)),
+            pl.BlockSpec((block, fresh.shape[1], kv_width), lambda i: (i, 0, 0)),
         ]
         + [pl.BlockSpec(memory_space=pl.ANY)] * len(earlier),
-        out_specs=pl.BlockSpec((n_steps, rows, HEADS * HD), lambda i: (0, c, 0)),
+        out_specs=pl.BlockSpec(
+            (n_steps, block, HEADS * HD), lambda i: (0, first_row // block + i, 0)
+        ),
         input_output_aliases={4: 0} if earlier else {},
         compiler_params=pltpu.CompilerParams(vmem_limit_bytes=40 * 1024 * 1024),
         cost_estimate=pl.CostEstimate(
@@ -172,12 +175,14 @@
     n_tensor = lax.axis_size("tensor")
     n_dp = lax.axis_size("dp")
     row_dev = lengths.shape[0]
-    chunks = 3 if row_dev % 3 == 0 else 1
-    row_chunk = row_dev // chunks
+    third = row_dev // 3
+    spans = [(i * third, third) for i in range(3)] if row_dev % 3 == 0 else [(0, row_dev)]
     group_index = lax.axis_index("dp")
 
     flat = hidden.reshape(n_steps * n_rows, width_dev)
-    relay = 2 < n_tensor <= 8
+    fresh = jnp.pad(new_kv.transpose(1, 0, 2), ((0, 0), (0, 16 - n_steps), (0, 0)))
+    fresh = [fresh[start : start + size] for start, size in spans]
+    relay = n_tensor == 4
     arrived = {}
     if relay:
         arrived[(1, -1)], arrived[(1, 1)] = hop_once(flat, flat, 1, n_tensor)
@@ -198,16 +203,16 @@
     ).reshape(n_dp, SLOTS, rank_size, col_count)
     n_slots = n_dp * SLOTS
     pages = [
-        kv_cache.at[page_table[c * row_chunk : (c + 1) * row_chunk].reshape(-1)]
+        kv_cache.at[page_table[start : start + size].reshape(-1)]
         .get(mode="promise_in_bounds")
-        .reshape(row_chunk, -1, kv_cache.shape[2])
-        for c in range(chunks)
+        .reshape(size, -1, kv_cache.shape[2])
+        for start, size in spans
     ]
     total = None
     if relay:
         total = block_dot(flat, w_query, lax.axis_index("tensor"))
-        far_left, far_right, pages, total, _ = lax.optimization_barrier(
-            (arrived[(1, -1)], arrived[(1, 1)], pages, total, b_send)
+        far_left, far_right, pages[0], total, _ = lax.optimization_barrier(
+            (arrived[(1, -1)], arrived[(1, 1)], pages[0], total, b_send)
         )
         arrived[(1, -1)], arrived[(1, 1)] = far_left, far_right
         arrived[(2, -1)], arrived[(2, 1)] = hop_once(far_left, far_right, 2, n_tensor)
@@ -230,40 +235,44 @@
     if relay:
         first, number = nth_block(arrived, 0, n_tensor)
         total = total + block_dot(first, w_query, number)
-        far_left, far_right = arrived[(2, -1)], arrived[(2, 1)]
-        far_left, far_right, total, low_part = lax.optimization_barrier(
-            (far_left, far_right, total, low_part)
+        fresh, pages[1:], total, low_part, far_left, far_right = lax.optimization_barrier(
+            (fresh, pages[1:], total, low_part, arrived[(2, -1)], arrived[(2, 1)])
         )
         arrived[(2, -1)], arrived[(2, 1)] = far_left, far_right
-        for hop in range(3, n_tensor):
-            far_left, far_right = hop_once(far_left, far_right, hop, n_tensor)
-            arrived[(hop, -1)], arrived[(hop, 1)] = far_left, far_right
+        me = lax.axis_index("tensor")
+        middle = jnp.where(
+            me == 1, far_right, jnp.where(me == 2, far_left, jnp.zeros((), far_left.dtype))
+        )
+        last = lax.ppermute(middle, "tensor", [(2, 3), (1, 0)])
+        last_number = jnp.where(me < 2, 3, 0)
     low_split = low_part.reshape(n_tensor, -1, rank_size)
     low_mine = jnp.sum(lax.all_to_all(low_split, "tensor", 0, 0), axis=0).astype(jnp.bfloat16)
-    low_bf = lax.all_gather(low_mine, "tensor", axis=0, tiled=True)
-    low_bf = low_bf.reshape(n_steps, n_rows, rank_size)
-    spread = jnp.where(onehot[None, :, :, None], low_bf[:, :, None, :], jnp.zeros((), jnp.bfloat16))
-    spread = spread.reshape(n_steps, n_tensor, row_dev, n_slots * rank_size)
-
-    delta = jnp.dot(
-        spread.reshape(-1, n_slots * rank_size), b_select, preferred_element_type=jnp.float32
-    )
     if relay:
         for k in range(1, n_tensor - 2):
             block, number = nth_block(arrived, k, n_tensor)
             total = total + block_dot(block, w_query, number)
+        total = total + block_dot(middle, w_query, last_number)
+    low_bf = lax.all_gather(low_mine, "tensor", axis=0, tiled=True)
+    low_bf = low_bf.reshape(n_steps, n_rows, rank_size)
+    if relay:
+        low_bf, total = lax.optimization_barrier((low_bf, total))
+    spread = jnp.where(onehot[None, :, :, None], low_bf[:, :, None, :], jnp.zeros((), jnp.bfloat16))
+    spread = spread.reshape(n_steps, n_tensor, row_dev, n_slots * rank_size)
+
+    delta = jnp.dot(
+        spread.reshape(-1, n_slots * rank_size), b_select, preferred_element_type=jnp.float32
+    )
+    if relay:
         total = total + delta
-        last, last_number = nth_block(arrived, n_tensor - 2, n_tensor)
     else:
         total, last, last_number = delta, lax.all_gather(flat, "tensor", axis=1, tiled=True), 0
     total = total.reshape(n_steps, n_tensor, row_dev, col_count)
     last = last.reshape(n_steps, n_tensor, row_dev, -1)
 
-    fresh = jnp.pad(new_kv.transpose(1, 0, 2), ((0, 0), (0, 16 - n_steps), (0, 0)))
     head_dev = col_count // HD
     outs, result = [], None
-    for c in range(chunks):
-        rows = slice(c * row_chunk, (c + 1) * row_chunk)
+    for c, (first_row, row_chunk) in enumerate(spans):
+        rows = slice(first_row, first_row + row_chunk)
         part = last[:, :, rows].reshape(-1, last.shape[3])
         q = block_dot(part, w_query, last_number) + total[:, :, rows].reshape(-1, col_count)
         q = q.astype(jnp.bfloat16)
@@ -272,10 +281,10 @@
         q = lax.all_to_all(q, "tensor", 0, 0, tiled=True)
         q = q.reshape(KVH, n_tensor // KVH, row_chunk, n_steps, head_dev, HD)
         q = q.transpose(0, 2, 3, 1, 4, 5).reshape(KVH, row_chunk, n_steps * SHARE, HD)
-        if row_chunk % 16 == 0:
-            result = attend_into(result, c, q, pages[c], fresh[rows], lengths[rows], row_dev)
+        if all(size % 16 == 0 for _, size in spans):
+            result = attend_into(result, first_row, q, pages[c], fresh[c], lengths[rows], row_dev)
         else:
-            out = attend(q, pages[c], fresh[rows], lengths[rows])
+            out = attend(q, pages[c], fresh[c], lengths[rows])
             out = out.reshape(KVH, row_chunk, n_steps, SHARE * HD).transpose(2, 1, 0, 3)
             outs.append(out.reshape(n_steps, row_chunk, HEADS * HD))
     return jnp.concatenate(outs, axis=1) if outs else result

time: 270 us -> 257 us (0.952)
  blocking collectives: 64.9 us -> 39.5 us
  matrix products: 35.8 us -> 43.1 us
  waiting for transfers between devices: 55.4 us -> 58.8 us
    all_gather x1, blocking collectives: 52.9 us -> 39.5 us  [on_device(): low_bf = lax.all_gather(low_mine, 'tensor', axis=0, tiled=True)]
    all_to_all x1 -> x0, blocking collectives: 12 us -> none  [on_device(): lax.all_to_all(low_split, 'tensor', 0, 0)]
    all_to_all x0 -> x1, waiting for transfers between devices: none -> 6.76 us  [on_device(): lax.all_to_all(low_split, 'tensor', 0, 0)]
    dot_general x6 -> x7, matrix products: 26.8 us -> 32.8 us  [block_dot(): return jnp.dot(block, w_block, preferred_element_type=jnp.float32)]
    all_to_all x1, waiting for transfers between devices: 5.6 us -> 1.9 us  [on_device(): lax.all_to_all(a_send, 'dp', 0, 0, tiled=True)]
    all_to_all x0 -> x1, starting transfers between devices: none -> 3.45 us  [on_device(): lax.all_to_all(low_split, 'tensor', 0, 0)]
    ppermute x3 -> x2, starting transfers between devices: 11.3 us -> 9.24 us  [hop_once(): lax.ppermute(from_left, 'tensor', right_pairs)]
    ppermute x3 -> x2, waiting for transfers between devices: 39.3 us -> 40.6 us  [hop_once(): lax.ppermute(from_right, 'tensor', left_pairs)]
  transfers between devices with their start and end apart: 11 -> 11, of which waited for: 4 -> 5; matrix products, arithmetic and copies ran while one was open for 31% -> 37% of each run, Pallas kernels for 3% -> 3%
where the time goes in v3:
time: 257 us; the launch traced here: 256 us
  waiting for transfers between devices  58.8 us (23%)
  local copies, waits for them, and re-layouts  50.1 us (19%)
  matrix products  43.1 us (17%)
  blocking collectives  39.5 us (15%)
  starting transfers between devices  37.5 us (15%)
  other arithmetic  14.5 us (6%)
  Pallas kernels  12.4 us (5%)
    ppermute x2, waiting for transfers between devices, hop_once(): lax.ppermute(from_right, 'tensor', left_pairs)  40.6 us
    all_gather x1, blocking collectives, on_device(): low_bf = lax.all_gather(low_mine, 'tensor', axis=0, tiled=True)  39.5 us
    dot_general x7, matrix products, block_dot(): return jnp.dot(block, w_block, preferred_element_type=jnp.float32)  32.8 us
    gather x3, local copies, waits for them, and re-layouts, on_device(): pages = [kv_cache.at[page_table[start:start + size].reshape(-1)].get(mode...  22.2 us
    pallas_call x3, Pallas kernels, attend_into(): pl.pallas_call(functools.partial(attend_kernel, store_columns), grid=(row...  12.4 us
    all_to_all x3, starting transfers between devices, on_device(): q = lax.all_to_all(q, 'tensor', 0, 0, tiled=True)  11.1 us
    all_to_all x3, waiting for transfers between devices, on_device(): q = lax.all_to_all(q, 'tensor', 0, 0, tiled=True)  9.54 us
    ppermute x2, starting transfers between devices, hop_once(): lax.ppermute(from_left, 'tensor', right_pairs)  9.24 us
  transfers between devices with their start and end apart: 11, of which 5 were waited for; matrix products, arithmetic and copies ran while one was open for 37% of the time, Pallas kernels for 3%

profile of v3, /device:TPU:0, one launch (start us, length us, event | category | flops | bytes accessed | tf_op | source)
XLA Modules:
  0.0 256.2 jit_solution(13125932382667462574)
XLA Ops:
  0.0 1.5 collective-permute-start.1
  1.6 7.0 %collective-permute-start = (bf16[576,2048]{1,0:T(8,128)(2,1)}, bf16[576,2048]{1,0:T(8,128)(2,1)}, u32[]{:S(2)}, u32[]{:S(2)}) collective-permute-start(bf16[576,2048]{1,0:T(8,128)(2,1)} %bitcast.118), channel_id=1, source_target_pairs={{0,1},{1,2},{2,3},{4,5},{5,6},{6,7},{8,9},{9,10},{10,11},{12,13},{... | collective-permute-start | bytes 7077896 | tf_op jit(solution)/shard_map/ppermute | solution.py:135
  8.6 0.7 fusion.77
  9.3 0.2 reduce_window_sum.11
  9.5 0.7 add_select_fusion
  10.2 0.1 select_reduce_fusion.2
  10.3 0.1 copy.34
  10.4 0.1 reshape.293
  10.5 1.5 gather_fusion.6
  12.1 5.8 %gather_fusion.5 = bf16[8,2048,128]{2,1,0:T(8,128)(2,1)} fusion(bf16[12,2048,128]{2,1,0:T(8,128)(2,1)} %param.14, s32[1024]{0:T(1024)S(1)} %pad_clamp_fusion), kind=kCustom, calls=%fused_computation.5 | custom fusion | bytes 8388640 | tf_op jit(solution)/shard_map/gather | solution.py:197
  17.9 5.8 %fusion = bf16[4,2,2048,128]{3,2,1,0:T(8,128)(2,1)} fusion(bf16[4,2,2048,128]{3,2,1,0:T(8,128)(2,1)} %bitcast.101, f32[4,2,2048]{2,1,0:T(2,128)S(1)} %mul.51), kind=kLoop, calls=%fused_computation.8 | loop fusion | flops 6291456 | bytes 8454144 | tf_op jit(solution)/shard_map/convert_element_type | solution.py:18
  23.7 5.0 %all-to-all-start = ((bf16[4,2,2048,128]{3,2,1,0:T(8,128)(2,1)}), bf16[4,2,2048,128]{3,2,1,0:T(8,128)(2,1)}, u32[]{:S(2)}, u32[]{:S(2)}) async-start(bf16[4,2,2048,128]{3,2,1,0:T(8,128)(2,1)} %fusion), calls=%async_computation | async-start | bytes 8388608 | tf_op jit(solution)/shard_map/all_to_all | solution.py:219
  28.7 0.6 gather_fusion.4
  29.5 0.6 reshape.291
  30.1 0.1 reshape.286
  30.3 0.1 reshape.288
  30.4 1.2 copy.55
  31.6 2.0 gather_fusion.3
  33.6 7.3 %gather_fusion.1 = bf16[128,16,1024]{2,1,0:T(8,128)(2,1)} fusion(bf16[384,16,1024]{2,1,0:T(8,128)(2,1)} %param.23, s32[1024]{0:T(1024)S(1)} %pad_clamp_fusion.2), kind=kCustom, calls=%fused_computation.1 | custom fusion | bytes 8389120 | tf_op jit(solution)/shard_map/gather | solution.py:207
  41.0 7.4 %gather_fusion = bf16[128,16,1024]{2,1,0:T(8,128)(2,1)} fusion(bf16[384,16,1024]{2,1,0:T(8,128)(2,1)} %param.23, s32[1024]{0:T(1024)S(1)} %pad_clamp_fusion.3), kind=kCustom, calls=%fused_computation | custom fusion | bytes 8389120 | tf_op jit(solution)/shard_map/gather | solution.py:207
  48.4 7.5 %gather_fusion.2 = bf16[128,16,1024]{2,1,0:T(8,128)(2,1)} fusion(bf16[384,16,1024]{2,1,0:T(8,128)(2,1)} %param.23, s32[1024]{0:T(1024)S(1)} %pad_clamp_fusion.1), kind=kCustom, calls=%fused_computation.2 | custom fusion | bytes 8389120 | tf_op jit(solution)/shard_map/gather | solution.py:207
  55.9 0.8 bitcast_select_fusion.1
  56.8 1.7 fusion.1
  58.5 4.4 %fusion.25 = f32[576,1024]{1,0:T(8,128)S(1)} fusion(bf16[576,2048]{1,0:T(8,128)(2,1)S(1)} %bitcast.119, bf16[8192,1024]{1,0:T(8,128)(2,1)} %param.13, s32[]{:T(128)S(6)} %select_n.166), kind=kOutput, calls=%fused_computation.40 | convolution fusion | flops 2415919104 | bytes 8912900 | tf_op jit(solution)/shard_map/dot_general | solution.py:128
  63.0 2.2 collective-permute-start.2
  65.2 1.3 collective-permute-start.3
  66.5 0.2 select_reduce_fusion.1
  66.7 0.1 select_reduce_fusion
  66.8 1.0 pad_slice_fusion
  67.8 5.1 %fusion.4 = f32[576,1024]{1,0:T(8,128)S(1)} fusion(bf16[8192,1024]{1,0:T(8,128)(2,1)} %param.13, s32[]{:T(128)S(6)} %select_n.174, bf16[576,2048]{1,0:T(8,128)(2,1)} %collective-permute-done.1, bf16[576,2048]{1,0:T(8,128)(2,1)} %collective-permute-done, pred[]{:T(512)S(6)} %eq.85), kind=kOutput, calls=%fused_computation.13 | convolution fusion | flops 2417098752 | bytes 11272197 | tf_op jit(solution)/shard_map/dot_general | solution.py:128
  73.0 2.1 add.137
  75.0 1.9 all-to-all-done
  76.9 6.3 %fusion.16 = f32[3,192,128]{2,1,0:T(8,128)} fusion(pred[192,8]{0,1:T(8,128)(4,1)S(1)} %iota_compare_fusion, bf16[8,2048,128,1]{2,1,3,0:T(8,128)(2,1)} %bitcast.20, bf16[3,192,2048]{2,1,0:T(8,128)(2,1)} %param.12), kind=kOutput, calls=%fused_computation.29 | convolution fusion | flops 2417025024 | bytes 6850048 | tf_op jit(solution)/shard_map/trd,kdc->trkc/dot_general | solution.py:233
  83.2 40.5 %collective-permute-done.3 = bf16[576,2048]{1,0:T(8,128)(2,1)} collective-permute-done((bf16[576,2048]{1,0:T(8,128)(2,1)}, bf16[576,2048]{1,0:T(8,128)(2,1)}, u32[]{:S(2)}, u32[]{:S(2)}) %collective-permute-start.3) | collective-permute-done | bytes 2359328 | tf_op jit(solution)/shard_map/ppermute | solution.py:136
  123.8 3.5 %all-to-all-start.1 = ((f32[4,144,128]{2,1,0:T(8,128)}), f32[4,144,128]{2,1,0:T(8,128)S(1)}, u32[]{:S(2)}, u32[]{:S(2)}) async-start(f32[4,144,128]{2,1,0:T(8,128)} %bitcast.25), calls=%async_computation.1 | async-start | bytes 589824 | tf_op jit(solution)/shard_map/all_to_all | solution.py:249
  127.2 1.7 select_select_fusion
  129.0 1.3 collective-permute-start.4
  130.2 6.8 %all-to-all-done.1 = f32[4,144,128]{2,1,0:T(8,128)S(1)} async-done(((f32[4,144,128]{2,1,0:T(8,128)}), f32[4,144,128]{2,1,0:T(8,128)S(1)}, u32[]{:S(2)}, u32[]{:S(2)}) %all-to-all-start.1) | async-done | bytes 294944 | tf_op jit(solution)/shard_map/all_to_all | solution.py:249
  137.0 4.6 %all-to-all-start.2 = ((bf16[4,2,128,1024]{3,2,1,0:T(8,128)(2,1)}), bf16[4,2,128,1024]{3,2,1,0:T(8,128)(2,1)}, u32[]{:S(2)}, u32[]{:S(2)}) async-start(bf16[4,2,128,1024]{3,2,1,0:T(8,128)(2,1)} %fusion.1), calls=%async_computation.2 | async-start | bytes 4194304 | tf_op jit(solution)/shard_map/all_to_all | solution.py:220
  141.6 6.0 %fusion.2 = f32[576,1024]{1,0:T(8,128)S(1)} fusion(bf16[8192,1024]{1,0:T(8,128)(2,1)} %param.13, s32[]{:T(128)S(6)} %select_n.191, bf16[576,2048]{1,0:T(8,128)(2,1)} %collective-permute-done.3, bf16[576,2048]{1,0:T(8,128)(2,1)} %collective-permute-done.2, bf16[576,2048]{1,0:T(8,128)(2,1)} %collective-permute-done.1, pred[]{:T(512)S(6)} %eq.97, pred[]{:T(512)S(6)} %eq.85), kind=kOutput, calls=%fused_computation.11 | convolution fusion | flops 2418278400 | bytes 13631494 | tf_op jit(solution)/shard_map/dot_general | solution.py:128
  147.7 6.9 %add_add_fusion = f32[576,1024]{1,0:T(8,128)} fusion(f32[576,1024]{1,0:T(8,128)S(1)} %copy-done.7, f32[576,1024]{1,0:T(8,128)S(1)} %fusion.2, bf16[576,2048]{1,0:T(8,128)(2,1)} %select_select_fusion, bf16[8192,1024]{1,0:T(8,128)(2,1)} %param.13, s32[]{:T(128)S(6)} %select_n.185), kind=kOutput, calls=%fused_computation.32 | convolution fusion | flops 2417098752 | bytes 13631492 | tf_op jit(solution)/shard_map/dot_general | solution.py:128
  154.6 39.5 %all_gather.3 = bf16[576,128]{1,0:T(8,128)(2,1)S(1)} all-gather(bf16[144,128]{1,0:T(8,128)(2,1)S(1)} %reduce_sum.52), channel_id=1, replica_groups=mesh['replica'=2,'dp'=4,'tensor'=4] {'tensor'}, dimensions={0}, use_global_device_ids=true | all-gather | bytes 184320 | tf_op jit(solution)/shard_map/all_gather | solution.py:255
  194.1 0.3 broadcast_select_fusion
  194.4 1.8 copy.35
  196.2 4.0 %convolution_add_fusion = f32[576,1024]{1,0:T(8,128)S(1)} fusion(f32[576,1024]{1,0:T(8,128)} %add_add_fusion, bf16[1024,1024]{1,0:T(8,128)(2,1)} %bitcast.27, bf16[72,8,8,128]{3,2,1,0:T(8,128)(2,1)} %bitcast.114), kind=kOutput, calls=%fused_computation.41 | convolution fusion | flops 1208549376 | bytes 7995392 | tf_op jit(solution)/shard_map/dot_general | solution.py:262
  200.3 1.0 fusion.80
  201.3 3.0 %fusion.79 = (bf16[3,4,16,2048]{3,2,1,0:T(8,128)(2,1)}, bf16[3,4,16,2048]{3,2,1,0:T(8,128)(2,1)S(1)}, bf16[3,4,16,2048]{3,2,1,0:T(8,128)(2,1)}) fusion(bf16[3,4,48,2048]{3,2,1,0:T(8,128)(2,1)} %bitcast.23), kind=kLoop, calls=%fused_computation.102 | loop fusion | bytes 4718592 | tf_op jit(solution)/shard_map/slice | solution.py:276
  204.3 3.2 %fusion.49 = bf16[24,8,8,128]{3,1,2,0:T(8,128)(2,1)S(1)} fusion(f32[192,1024]{1,0:T(8,128)S(1)} %bitcast.107, bf16[192,2048]{1,0:T(8,128)(2,1)S(1)} %bitcast.108, bf16[8192,1024]{1,0:T(8,128)(2,1)} %param.13, s32[]{:T(128)S(6)} %select_n.185), kind=kOutput, calls=%fused_computation.49 | convolution fusion | flops 805699584 | bytes 6160388 | tf_op jit(solution)/shard_map/dot_general | solution.py:128
  207.6 0.8 copy.53
  208.4 3.9 %all-to-all-start.4 = ((bf16[4,16,24,128]{3,2,1,0:T(8,128)(2,1)}), bf16[4,16,24,128]{3,2,1,0:T(8,128)(2,1)S(1)}, u32[]{:S(2)}, u32[]{:S(2)}) async-start(bf16[4,16,24,128]{3,2,1,0:T(8,128)(2,1)} %bitcast.95), calls=%async_computation.4 | async-start | bytes 786432 | tf_op jit(solution)/shard_map/all_to_all | solution.py:281
  212.4 3.6 %fusion.52 = bf16[24,8,8,128]{3,1,2,0:T(8,128)(2,1)S(1)} fusion(f32[192,1024]{1,0:T(8,128)} %bitcast.105, bf16[192,2048]{1,0:T(8,128)(2,1)} %bitcast.106, bf16[8192,1024]{1,0:T(8,128)(2,1)} %param.13, s32[]{:T(128)S(6)} %select_n.185), kind=kOutput, calls=%fused_computation.50 | convolution fusion | flops 805699584 | bytes 6160388 | tf_op jit(solution)/shard_map/dot_general | solution.py:128
  216.0 0.8 copy.52
  216.9 4.8 %all-to-all-done.4.q_ref = bf16[4,16,24,128]{3,2,1,0:T(8,128)(2,1)S(1)} async-done(((bf16[4,16,24,128]{3,2,1,0:T(8,128)(2,1)}), bf16[4,16,24,128]{3,2,1,0:T(8,128)(2,1)S(1)}, u32[]{:S(2)}, u32[]{:S(2)}) %all-to-all-start.4) | async-done | bytes 393248 | tf_op jit(solution)/shard_map/all_to_all | solution.py:281
  221.6 3.5 %all-to-all-start.5 = ((bf16[4,16,24,128]{3,2,1,0:T(8,128)(2,1)}), bf16[4,16,24,128]{3,2,1,0:T(8,128)(2,1)S(1)}, u32[]{:S(2)}, u32[]{:S(2)}) async-start(bf16[4,16,24,128]{3,2,1,0:T(8,128)(2,1)} %bitcast.94), calls=%async_computation.5 | async-start | bytes 786432 | tf_op jit(solution)/shard_map/all_to_all | solution.py:281
  225.1 3.4 %fusion.46 = bf16[24,8,8,128]{3,1,2,0:T(8,128)(2,1)S(1)} fusion(f32[192,1024]{1,0:T(8,128)S(1)} %bitcast.103, bf16[192,2048]{1,0:T(8,128)(2,1)} %bitcast.104, bf16[8192,1024]{1,0:T(8,128)(2,1)} %param.13, s32[]{:T(128)S(6)} %select_n.185), kind=kOutput, calls=%fused_computation.48 | convolution fusion | flops 805699584 | bytes 6160388 | tf_op jit(solution)/shard_map/dot_general | solution.py:128
  228.6 0.8 copy.54
  229.4 4.8 %all-to-all-done.5.q_ref = bf16[4,16,24,128]{3,2,1,0:T(8,128)(2,1)S(1)} async-done(((bf16[4,16,24,128]{3,2,1,0:T(8,128)(2,1)}), bf16[4,16,24,128]{3,2,1,0:T(8,128)(2,1)S(1)}, u32[]{:S(2)}, u32[]{:S(2)}) %all-to-all-start.5) | async-done | bytes 393248 | tf_op jit(solution)/shard_map/all_to_all | solution.py:281
  234.2 3.7 %all-to-all-start.3 = ((bf16[4,16,24,128]{3,2,1,0:T(8,128)(2,1)}), bf16[4,16,24,128]{3,2,1,0:T(8,128)(2,1)S(1)}, u32[]{:S(2)}, u32[]{:S(2)}) async-start(bf16[4,16,24,128]{3,2,1,0:T(8,128)(2,1)} %bitcast.96), calls=%async_computation.3 | async-start | bytes 786432 | tf_op jit(solution)/shard_map/all_to_all | solution.py:281
  238.1 2.2 copy-done.4
  240.3 4.1 %shard_map.118.refs_0_ = bf16[3,48,4096]{2,1,0:T(8,128)(2,1)} custom-call(s32[16,1,128]{2,1,0:T(1,128)S(1)} %broadcast_in_dim.122.len_ref, bf16[4,16,24,128]{3,2,1,0:T(8,128)(2,1)S(1)} %all-to-all-done.5.q_ref, bf16[16,128,1024]{2,1,0:T(8,128)(2,1)S(1)} %bitcast.100, bf16[16,16,1024]{2,1,0:T(8,128)(2,1)S(1)} %get-tuple-element.34.new_ref), custom_call_target="tpu_custom_call" | custom-call | flops 100663296 | bytes 4980736 | tf_op jit(solution)/shard_map/pallas_call | solution.py:75
  244.5 4.1 %shard_map.119.refs_0_ = bf16[3,48,4096]{2,1,0:T(8,128)(2,1)} custom-call(s32[16,1,128]{2,1,0:T(1,128)S(1)} %broadcast_in_dim.121.len_ref, bf16[4,16,24,128]{3,2,1,0:T(8,128)(2,1)S(1)} %all-to-all-done.4.q_ref, bf16[16,128,1024]{2,1,0:T(8,128)(2,1)S(1)} %bitcast.99, ...), custom_call_target="tpu_custom_call", output_to_operand_aliasing={{}: (4, {})} | custom-call | flops 100663296 | bytes 4980736 | tf_op jit(solution)/shard_map/pallas_call | solution.py:75
  248.7 2.3 copy-done.2
  251.1 1.0 copy-done.5
  252.1 4.1 %shard_map.120 = bf16[3,48,4096]{2,1,0:T(8,128)(2,1)} custom-call(s32[16,1,128]{2,1,0:T(1,128)S(1)} %broadcast_in_dim.72.len_ref, bf16[4,16,24,128]{3,2,1,0:T(8,128)(2,1)S(1)} %all-to-all-done.3.q_ref, bf16[16,128,1024]{2,1,0:T(8,128)(2,1)S(1)} %bitcast.98, bf16[16,16,1024]{2,1,0:T(8,128)(2,1)S(1)} %copy-done.5, ...), custom_call_target="tpu_custom_call", output_to_operand_aliasing={{}: (4, {})} | custom-call | flops 100663296 | bytes 4980736 | tf_op jit(solution)/shard_map/pallas_call | solution.py:75
  (54 shorter events, 1.0 us)
Async XLA Ops:
  0.0 31.6 %copy-start = (bf16[12,128,1024]{2,1,0:T(8,128)(2,1)S(1)}, bf16[12,128,1024]{2,1,0:T(8,128)(2,1)}, u32[]{:S(2)}) copy-start(bf16[12,128,1024]{2,1,0:T(8,128)(2,1)} %param.16) | copy-start | bytes 9437188
  0.0 63.0 %collective-permute-start.1 = (bf16[576,2048]{1,0:T(8,128)(2,1)}, bf16[576,2048]{1,0:T(8,128)(2,1)}, u32[]{:S(2)}, u32[]{:S(2)}) collective-permute-start(bf16[576,2048]{1,0:T(8,128)(2,1)} %bitcast.117), channel_id=1, source_target_pairs={{1,0},{2,1},{3,2},{5,4},{6,5},{7,6},{9,8},{10,9},{11,10},{13,12},{... | collective-permute-start | bytes 7077896 | tf_op jit(solution)/shard_map/ppermute | solution.py:136
  1.6 61.4 %collective-permute-start = (bf16[576,2048]{1,0:T(8,128)(2,1)}, bf16[576,2048]{1,0:T(8,128)(2,1)}, u32[]{:S(2)}, u32[]{:S(2)}) collective-permute-start(bf16[576,2048]{1,0:T(8,128)(2,1)} %bitcast.118), channel_id=1, source_target_pairs={{0,1},{1,2},{2,3},{4,5},{5,6},{6,7},{8,9},{9,10},{10,11},{12,13},{... | collective-permute-start | bytes 7077896 | tf_op jit(solution)/shard_map/ppermute | solution.py:135
  23.7 5.1 %copy-start.8 = (f32[12,128]{1,0:T(8,128)S(1)}, f32[12,128]{1,0:T(8,128)}, u32[]{:S(2)}) copy-start(f32[12,128]{1,0:T(8,128)} %param.17) | copy-start | bytes 18436
  23.7 5.6 %copy-start.9 = (s32[48,8]{0,1:T(8,128)S(1)}, s32[48,8]{0,1:T(8,128)}, u32[]{:S(2)}) copy-start(s32[48,8]{0,1:T(8,128)} %param.21) | copy-start | bytes 4612
  23.7 53.2 %all-to-all-start = ((bf16[4,2,2048,128]{3,2,1,0:T(8,128)(2,1)}), bf16[4,2,2048,128]{3,2,1,0:T(8,128)(2,1)}, u32[]{:S(2)}, u32[]{:S(2)}) async-start(bf16[4,2,2048,128]{3,2,1,0:T(8,128)(2,1)} %fusion), calls=%async_computation | async-start | bytes 8388608 | tf_op jit(solution)/shard_map/all_to_all | solution.py:219
  41.0 7.4 %copy-start.12 = (s32[128,1]{0,1:T(1,128)S(1)}, s32[128,1]{0,1:T(1,128)}, u32[]{:S(2)}) copy-start(s32[128,1]{0,1:T(1,128)} %reshape.291) | copy-start | bytes 1540
  48.4 8.4 %copy-start.6 = (bf16[8,128,1024]{2,1,0:T(8,128)(2,1)S(1)}, bf16[8,128,1024]{2,1,0:T(8,128)(2,1)}, u32[]{:S(2)}) copy-start(bf16[8,128,1024]{2,1,0:T(8,128)(2,1)} %gather_fusion.3) | copy-start | bytes 6291460
  55.9 2.6 %copy-start.13 = (bf16[3,192,2048]{2,1,0:T(8,128)(2,1)S(1)}, bf16[3,192,2048]{2,1,0:T(8,128)(2,1)}, u32[]{:S(2)}) copy-start(bf16[3,192,2048]{2,1,0:T(8,128)(2,1)} %param.12) | copy-start | bytes 7077892
  58.5 8.2 %copy-start.11 = (s32[192]{0:T(256)S(1)}, s32[192]{0:T(256)}, u32[]{:S(2)}) copy-start(s32[192]{0:T(256)} %param.19) | copy-start | bytes 2308
  63.0 20.2 %collective-permute-start.2 = (bf16[576,2048]{1,0:T(8,128)(2,1)}, bf16[576,2048]{1,0:T(8,128)(2,1)}, u32[]{:S(2)}, u32[]{:S(2)}) collective-permute-start(bf16[576,2048]{1,0:T(8,128)(2,1)} %collective-permute-done), channel_id=1, source_target_pairs={{1,2},{2,3},{5,6},{6,7},{9,10},{10,11},{13,14},{14,15},{17,18},{18... | collective-permute-start | bytes 7077896 | tf_op jit(solution)/shard_map/ppermute | solution.py:135
  65.2 58.6 %collective-permute-start.3 = (bf16[576,2048]{1,0:T(8,128)(2,1)}, bf16[576,2048]{1,0:T(8,128)(2,1)}, u32[]{:S(2)}, u32[]{:S(2)}) collective-permute-start(bf16[576,2048]{1,0:T(8,128)(2,1)} %collective-permute-done.1), channel_id=1, source_target_pairs={{1,0},{2,1},{5,4},{6,5},{9,8},{10,9},{13,12},{14,13},{17,16},{18,1... | collective-permute-start | bytes 7077896 | tf_op jit(solution)/shard_map/ppermute | solution.py:136
  123.8 13.2 %all-to-all-start.1 = ((f32[4,144,128]{2,1,0:T(8,128)}), f32[4,144,128]{2,1,0:T(8,128)S(1)}, u32[]{:S(2)}, u32[]{:S(2)}) async-start(f32[4,144,128]{2,1,0:T(8,128)} %bitcast.25), calls=%async_computation.1 | async-start | bytes 589824 | tf_op jit(solution)/shard_map/all_to_all | solution.py:249
  129.0 72.3 %collective-permute-start.4 = (bf16[576,2048]{1,0:T(8,128)(2,1)}, bf16[576,2048]{1,0:T(8,128)(2,1)}, u32[]{:S(2)}, u32[]{:S(2)}) collective-permute-start(bf16[576,2048]{1,0:T(8,128)(2,1)} %select_select_fusion), channel_id=1, source_target_pairs={{2,3},{1,0},{6,7},{5,4},{10,11},{9,8},{14,15},{13,12},{18,19},{17,... | collective-permute-start | bytes 7077896 | tf_op jit(solution)/shard_map/ppermute | solution.py:246
  137.0 59.2 %all-to-all-start.2 = ((bf16[4,2,128,1024]{3,2,1,0:T(8,128)(2,1)}), bf16[4,2,128,1024]{3,2,1,0:T(8,128)(2,1)}, u32[]{:S(2)}, u32[]{:S(2)}) async-start(bf16[4,2,128,1024]{3,2,1,0:T(8,128)(2,1)} %fusion.1), calls=%async_computation.2 | async-start | bytes 4194304 | tf_op jit(solution)/shard_map/all_to_all | solution.py:220
  141.6 6.0 %copy-start.7 = (f32[576,1024]{1,0:T(8,128)S(1)}, f32[576,1024]{1,0:T(8,128)}, u32[]{:S(2)}) copy-start(f32[576,1024]{1,0:T(8,128)} %add.137) | copy-start | bytes 7077892
  208.4 13.2 %all-to-all-start.4 = ((bf16[4,16,24,128]{3,2,1,0:T(8,128)(2,1)}), bf16[4,16,24,128]{3,2,1,0:T(8,128)(2,1)S(1)}, u32[]{:S(2)}, u32[]{:S(2)}) async-start(bf16[4,16,24,128]{3,2,1,0:T(8,128)(2,1)} %bitcast.95), calls=%async_computation.4 | async-start | bytes 786432 | tf_op jit(solution)/shard_map/all_to_all | solution.py:281
  221.6 12.6 %all-to-all-start.5 = ((bf16[4,16,24,128]{3,2,1,0:T(8,128)(2,1)}), bf16[4,16,24,128]{3,2,1,0:T(8,128)(2,1)S(1)}, u32[]{:S(2)}, u32[]{:S(2)}) async-start(bf16[4,16,24,128]{3,2,1,0:T(8,128)(2,1)} %bitcast.94), calls=%async_computation.5 | async-start | bytes 786432 | tf_op jit(solution)/shard_map/all_to_all | solution.py:281
  228.5 9.4 %copy-start.10 = (s32[48]{0:T(128)S(1)}, s32[48]{0:T(128)}, u32[]{:S(2)}) copy-start(s32[48]{0:T(128)} %param.20) | copy-start | bytes 580
  234.2 14.4 %all-to-all-start.3 = ((bf16[4,16,24,128]{3,2,1,0:T(8,128)(2,1)}), bf16[4,16,24,128]{3,2,1,0:T(8,128)(2,1)S(1)}, u32[]{:S(2)}, u32[]{:S(2)}) async-start(bf16[4,16,24,128]{3,2,1,0:T(8,128)(2,1)} %bitcast.96), calls=%async_computation.3 | async-start | bytes 786432 | tf_op jit(solution)/shard_map/all_to_all | solution.py:281
  238.1 2.2 copy-start.4
  240.3 4.2 %copy-start.3 = (bf16[128,16,1024]{2,1,0:T(8,128)(2,1)S(1)}, bf16[128,16,1024]{2,1,0:T(8,128)(2,1)}, u32[]{:S(2)}) copy-start(bf16[128,16,1024]{2,1,0:T(8,128)(2,1)} %gather_fusion) | copy-start | bytes 12582916
  248.6 7.6 %copy-start.1 = (bf16[12,128,1024]{2,1,0:T(8,128)(2,1)S(1)}, bf16[12,128,1024]{2,1,0:T(8,128)(2,1)}, u32[]{:S(2)}) copy-start(bf16[12,128,1024]{2,1,0:T(8,128)(2,1)} %param.16) | copy-start | bytes 9437188
  248.7 2.4 copy-start.2
  251.1 1.0 copy-start.5
